TPU v7x, 512 devices: a whole 4x4x16 slice. The times are simulated.
512 devices in a mesh: gx: 32 (over z_lo, y), gy: 16 (over x, z_hi, core).
Axes of the slice: x: 4, y: 4, z: 16 (z_hi: 2, z_lo: 8; z = z_hi * 8 + z_lo), core: 2. Of those that a mesh axis runs over, the one named last changes fastest.
Arguments:
- velocity: float32 [64, 256, 2048], P('gy', 'gx'), may hold values from -6 to 6
Outputs:
- coefficients: float32 [64, 256, 2048], P(None, 'gx', 'gy')
All inputs are finite; a program needn't handle non-finite values.
Results may differ from a plain program's by a relative error of at most 0.00007.
Values sent between devices are 32-bit elements; how exact they have to be, the bound alone decides.
A program may use at most 64 MiB of HBM per device.

v0:
```python
import jax
import jax.numpy as jnp
from jax import lax
from jax.sharding import PartitionSpec as P

PREDICT_FIRST = -1.586134342
UPDATE_FIRST = -0.05298011854
PREDICT_SECOND = 0.8829110762
UPDATE_SECOND = 0.4435068522
SCALE_LOW = 1.149604398
SCALE_HIGH = 1.0 / 1.149604398
EXACT = lax.Precision.HIGHEST


def with_halo(shard, sides, width):
    for axis, dim in sides:
        devices, length = (lax.axis_size(axis), shard.shape[dim])
        up = [(i, (i + 1) % devices) for i in range(devices)]
        down = [(j, i) for i, j in up]
        last = lax.slice_in_dim(shard, length - width, length, axis=dim)
        first = lax.slice_in_dim(shard, 0, width, axis=dim)
        before = lax.ppermute(last, axis, up)
        after = lax.ppermute(first, axis, down)
        shard = jnp.concatenate([before, shard, after], axis=dim)
    return shard


def split_pairs(values, which_dim):
    length = values.shape[which_dim]
    even_part = lax.slice_in_dim(values, 0, length, 2, which_dim)
    odd_part = lax.slice_in_dim(values, 1, length, 2, which_dim)
    return (even_part, odd_part)


def lifting_steps(even_part, odd_part, which_dim):
    odd_part = odd_part + PREDICT_FIRST * (even_part + jnp.roll(even_part, -1, which_dim))
    even_part = even_part + UPDATE_FIRST * (odd_part + jnp.roll(odd_part, 1, which_dim))
    odd_part = odd_part + PREDICT_SECOND * (even_part + jnp.roll(even_part, -1, which_dim))
    even_part = even_part + UPDATE_SECOND * (odd_part + jnp.roll(odd_part, 1, which_dim))
    return (even_part * SCALE_LOW, odd_part * SCALE_HIGH)


def join_pairs(even_part, odd_part, which_dim):
    stacked = jnp.stack((even_part, odd_part), axis=which_dim + 1)
    new_shape = list(even_part.shape)
    new_shape[which_dim] = new_shape[which_dim] * 2
    return stacked.reshape(new_shape)


def lift_periodic(values, which_dim):
    even_part, odd_part = split_pairs(values, which_dim)
    even_part, odd_part = lifting_steps(even_part, odd_part, which_dim)
    return join_pairs(even_part, odd_part, which_dim)


def lift_with_rim(extended, which_dim):
    even_part, odd_part = split_pairs(extended, which_dim)
    even_part, odd_part = lifting_steps(even_part, odd_part, which_dim)
    pair_count = even_part.shape[which_dim]
    even_part = lax.slice_in_dim(even_part, 2, pair_count - 2, 1, which_dim)
    odd_part = lax.slice_in_dim(odd_part, 2, pair_count - 2, 1, which_dim)
    return join_pairs(even_part, odd_part, which_dim)


def first_rim(matrix):
    return lift_with_rim(matrix, 0)


def second_rim(matrix):
    lifted = lift_with_rim(matrix[::2], 0)
    inner = matrix[8:-8]
    return inner.at[::2].set(lifted)


def second_whole(matrix):
    return matrix.at[::2].set(lift_periodic(matrix[::2], 0))


def make_table(extent, builder):
    identity = jnp.eye(extent, dtype=jnp.float32)
    return builder(identity).T


def apply_table(values, table, which_dim):
    if which_dim == 2:
        return jnp.dot(values, table, precision=EXACT)
    if which_dim == 1:
        return jnp.einsum("zey,ei->ziy", values, table, precision=EXACT)
    return jnp.einsum("exy,ei->ixy", values, table, precision=EXACT)


def is_even(length):
    return lax.broadcasted_iota(jnp.int32, (length,), 0) % 2 == 0


def body(velocity):
    depth = velocity.shape[0] * lax.axis_size("gy")
    width_x = velocity.shape[1]
    width_y = velocity.shape[2] // lax.axis_size("gy")
    tile_block = lax.all_to_all(velocity, "gy", split_axis=2, concat_axis=0, tiled=True)
    y_extended = with_halo(tile_block, (("gy", 2),), 4)
    tile_block = apply_table(y_extended, make_table(width_y + 8, first_rim), 2)
    x_extended = with_halo(tile_block, (("gx", 1),), 4)
    tile_block = apply_table(x_extended, make_table(width_x + 8, first_rim), 1)
    level_one = apply_table(tile_block, make_table(depth, lift_periodic_rows), 0)
    even_z = is_even(depth)[:, None, None]
    even_x = is_even(width_x)[None, :, None]
    even_y = is_even(width_y)[None, None, :]
    y_second = make_table(width_y + 16, second_rim)
    x_second = make_table(width_x + 16, second_rim)
    coarse_wide_y = with_halo(level_one, (("gy", 2),), 8)
    y_done = jnp.where(even_z & even_x, apply_table(coarse_wide_y, y_second, 2), level_one)
    coarse_wide_x = with_halo(y_done, (("gx", 1),), 8)
    x_done = jnp.where(even_z & even_y, apply_table(coarse_wide_x, x_second, 1), y_done)
    z_done = apply_table(x_done, make_table(depth, second_whole), 0)
    return jnp.where(even_x & even_y, z_done, x_done)


def lift_periodic_rows(matrix):
    return lift_periodic(matrix, 0)


def solution(mesh):
    in_specs = (P("gy", "gx", None),)
    out_specs = P(None, "gx", "gy")
    return jax.shard_map(body, mesh=mesh, in_specs=in_specs, out_specs=out_specs, check_vma=False)
```

profile of v0, /device:TPU:6, one launch (start us, length us, event | category | flops | bytes accessed | tf_op | source)
XLA Modules:
  0.0 169.5 jit_solution(13299550448670859749)
XLA Ops:
  0.0 4.3 %copy.32 = f32[4,8,2048]{1,0,2:T(4,128)} copy(f32[4,8,2048]{2,1,0:T(8,128)} %param.1) | data formatting | bytes 524288 | tf_op args[0]
  4.3 7.2 %reshape.183 = f32[16,1,4096]{2,1,0:T(1,128)} reshape(f32[2048,4,8]{2,1,0:T(4,128)} %bitcast.79) | data formatting | bytes 524288
  11.5 18.0 %all-to-all-start = ((f32[16,1,4096]{2,1,0:T(1,128)}), f32[16,1,4096]{2,1,0:T(1,128)S(1)}, u32[]{:S(2)}, u32[]{:S(2)}) async-start(f32[16,1,4096]{2,1,0:T(1,128)} %reshape.183), calls=%async_computation | async-start | bytes 524288 | tf_op jit(solution)/shard_map/all_to_all | solution.py:100
  31.1 13.4 %all-to-all-done = f32[16,1,4096]{2,1,0:T(1,128)S(1)} async-done(((f32[16,1,4096]{2,1,0:T(1,128)}), f32[16,1,4096]{2,1,0:T(1,128)S(1)}, u32[]{:S(2)}, u32[]{:S(2)}) %all-to-all-start) | async-done | bytes 262176 | tf_op jit(solution)/shard_map/all_to_all | solution.py:100
  44.6 0.5 broadcast.159
  45.1 1.3 reduce
  46.4 6.3 %reshape.184 = f32[2048,4,8]{2,1,0:T(4,128)} reshape(f32[16,4096]{1,0:T(8,128)S(1)} %reduce) | data formatting | bytes 524288
  52.7 3.4 %copy.33 = f32[4,8,16,128]{3,1,0,2:T(8,128)S(1)} copy(f32[4,8,16,128]{1,0,3,2:T(4,128)} %bitcast.78) | data formatting | bytes 524288 | tf_op jit(solution)/shard_map/all_to_all | solution.py:100
  56.2 2.1 %collective-permute-start.1 = (f32[64,8,4]{2,1,0:T(8,128)S(1)}, f32[64,8,4]{2,1,0:T(8,128)S(1)}, u32[]{:S(2)}, u32[]{:S(2)}) collective-permute-start(f32[64,8,4]{2,1,0:T(8,128)S(1)} %get-tuple-element.18), channel_id=1, source_target_pairs={{1,0},{2,1},{3,2},{4,3},{5,4},{6,5},{7,6},{8,7},{9,8},{10,9},{11,1... | collective-permute-start | bytes 24584 | tf_op jit(solution)/shard_map/ppermute | solution.py:23
  58.3 2.2 %collective-permute-start = (f32[64,8,4]{2,1,0:T(8,128)S(1)}, f32[64,8,4]{2,1,0:T(8,128)S(1)}, u32[]{:S(2)}, u32[]{:S(2)}) collective-permute-start(f32[64,8,4]{2,1,0:T(8,128)S(1)} %get-tuple-element.17), channel_id=1, source_target_pairs={{0,1},{1,2},{2,3},{3,4},{4,5},{5,6},{6,7},{7,8},{8,9},{9,10},{10,1... | collective-permute-start | bytes 24584 | tf_op jit(solution)/shard_map/ppermute | solution.py:22
  60.8 1.4 collective-permute-done.1
  62.2 29.6 %collective-permute-done = f32[64,8,4]{2,1,0:T(8,128)S(1)} collective-permute-done((f32[64,8,4]{2,1,0:T(8,128)S(1)}, f32[64,8,4]{2,1,0:T(8,128)S(1)}, u32[]{:S(2)}, u32[]{:S(2)}) %collective-permute-start) | collective-permute-done | bytes 8224 | tf_op jit(solution)/shard_map/ppermute | solution.py:22
  91.8 0.7 fusion.2
  92.6 8.2 %collective-permute-start.3 = (f32[64,4,128]{2,1,0:T(4,128)S(1)}, f32[64,4,128]{2,1,0:T(4,128)S(1)}, u32[]{:S(2)}, u32[]{:S(2)}) collective-permute-start(f32[64,4,128]{2,1,0:T(4,128)S(1)} %get-tuple-element.16), channel_id=1, source_target_pairs={{16,0},{32,16},{48,32},{64,48},{80,64},{96,80},{112,96},{128,112},... | collective-permute-start | bytes 393224 | tf_op jit(solution)/shard_map/ppermute | solution.py:23
  100.8 1.9 %collective-permute-start.2 = (f32[64,4,128]{2,1,0:T(4,128)S(1)}, f32[64,4,128]{2,1,0:T(4,128)S(1)}, u32[]{:S(2)}, u32[]{:S(2)}) collective-permute-start(f32[64,4,128]{2,1,0:T(4,128)S(1)} %get-tuple-element.15), channel_id=1, source_target_pairs={{0,16},{16,32},{32,48},{48,64},{64,80},{80,96},{96,112},{112,128},... | collective-permute-start | bytes 393224 | tf_op jit(solution)/shard_map/ppermute | solution.py:22
  102.8 0.5 collective-permute-done.3
  103.3 13.4 %collective-permute-done.2 = f32[64,4,128]{2,1,0:T(4,128)S(1)} collective-permute-done((f32[64,4,128]{2,1,0:T(4,128)S(1)}, f32[64,4,128]{2,1,0:T(4,128)S(1)}, u32[]{:S(2)}, u32[]{:S(2)}) %collective-permute-start.2) | collective-permute-done | bytes 131104 | tf_op jit(solution)/shard_map/ppermute | solution.py:22
  116.6 0.4 convolution_bitcast_fusion
  117.6 1.9 %collective-permute-start.5 = (f32[64,8,8]{2,0,1:T(8,128)S(1)}, f32[64,8,8]{2,0,1:T(8,128)S(1)}, u32[]{:S(2)}, u32[]{:S(2)}) collective-permute-start(f32[64,8,8]{2,0,1:T(8,128)S(1)} %get-tuple-element.14), channel_id=1, source_target_pairs={{1,0},{2,1},{3,2},{4,3},{5,4},{6,5},{7,6},{8,7},{9,8},{10,9},{11,1... | collective-permute-start | bytes 49160 | tf_op jit(solution)/shard_map/ppermute | solution.py:23
  119.6 2.4 %collective-permute-start.4 = (f32[64,8,8]{2,0,1:T(8,128)S(1)}, f32[64,8,8]{2,0,1:T(8,128)S(1)}, u32[]{:S(2)}, u32[]{:S(2)}) collective-permute-start(f32[64,8,8]{2,0,1:T(8,128)S(1)} %get-tuple-element.13), channel_id=1, source_target_pairs={{0,1},{1,2},{2,3},{3,4},{4,5},{5,6},{6,7},{7,8},{8,9},{9,10},{10,1... | collective-permute-start | bytes 49160 | tf_op jit(solution)/shard_map/ppermute | solution.py:22
  122.1 0.9 scatter_fusion.2
  123.0 12.7 %collective-permute-done.5 = f32[64,8,8]{2,0,1:T(8,128)S(1)} collective-permute-done((f32[64,8,8]{2,0,1:T(8,128)S(1)}, f32[64,8,8]{2,0,1:T(8,128)S(1)}, u32[]{:S(2)}, u32[]{:S(2)}) %collective-permute-start.5) | collective-permute-done | bytes 16416 | tf_op jit(solution)/shard_map/ppermute | solution.py:23
  135.7 8.3 %collective-permute-done.4 = f32[64,8,8]{2,0,1:T(8,128)S(1)} collective-permute-done((f32[64,8,8]{2,0,1:T(8,128)S(1)}, f32[64,8,8]{2,0,1:T(8,128)S(1)}, u32[]{:S(2)}, u32[]{:S(2)}) %collective-permute-start.4) | collective-permute-done | bytes 16416 | tf_op jit(solution)/shard_map/ppermute | solution.py:22
  144.1 0.7 convolution_select_fusion.1
  144.7 3.3 %collective-permute-start.7 = (f32[64,8,128]{2,0,1:T(8,128)S(1)}, f32[64,8,128]{2,0,1:T(8,128)S(1)}, u32[]{:S(2)}, u32[]{:S(2)}) collective-permute-start(f32[64,8,128]{2,0,1:T(8,128)S(1)} %convolution_select_fusion.1), channel_id=1, source_target_pairs={{16,0},{32,16},{48,32},{64,48},{80,64},{96,80},{112,96},{128,112},... | collective-permute-start | bytes 786440 | tf_op jit(solution)/shard_map/ppermute | solution.py:23
  148.1 2.5 %collective-permute-start.6 = (f32[64,8,128]{2,0,1:T(8,128)S(1)}, f32[64,8,128]{2,0,1:T(8,128)S(1)}, u32[]{:S(2)}, u32[]{:S(2)}) collective-permute-start(f32[64,8,128]{2,0,1:T(8,128)S(1)} %convolution_select_fusion.1), channel_id=1, source_target_pairs={{0,16},{16,32},{32,48},{48,64},{64,80},{80,96},{96,112},{112,128},... | collective-permute-start | bytes 786440 | tf_op jit(solution)/shard_map/ppermute | solution.py:22
  150.7 0.7 scatter_fusion
  151.4 0.6 scatter_fusion.1
  152.1 2.3 %collective-permute-done.7 = f32[64,8,128]{2,0,1:T(8,128)S(1)} collective-permute-done((f32[64,8,128]{2,0,1:T(8,128)S(1)}, f32[64,8,128]{2,0,1:T(8,128)S(1)}, u32[]{:S(2)}, u32[]{:S(2)}) %collective-permute-start.7) | collective-permute-done | bytes 262176 | tf_op jit(solution)/shard_map/ppermute | solution.py:23
  154.4 12.8 %collective-permute-done.6 = f32[64,8,128]{2,0,1:T(8,128)S(1)} collective-permute-done((f32[64,8,128]{2,0,1:T(8,128)S(1)}, f32[64,8,128]{2,0,1:T(8,128)S(1)}, u32[]{:S(2)}, u32[]{:S(2)}) %collective-permute-start.6) | collective-permute-done | bytes 262176 | tf_op jit(solution)/shard_map/ppermute | solution.py:22
  167.3 0.9 fusion
  168.6 0.9 copy.43
  (112 shorter events, 2.7 us)
Async XLA Ops:
  11.5 33.1 %all-to-all-start = ((f32[16,1,4096]{2,1,0:T(1,128)}), f32[16,1,4096]{2,1,0:T(1,128)S(1)}, u32[]{:S(2)}, u32[]{:S(2)}) async-start(f32[16,1,4096]{2,1,0:T(1,128)} %reshape.183), calls=%async_computation | async-start | bytes 524288 | tf_op jit(solution)/shard_map/all_to_all | solution.py:100
  56.2 6.0 %collective-permute-start.1 = (f32[64,8,4]{2,1,0:T(8,128)S(1)}, f32[64,8,4]{2,1,0:T(8,128)S(1)}, u32[]{:S(2)}, u32[]{:S(2)}) collective-permute-start(f32[64,8,4]{2,1,0:T(8,128)S(1)} %get-tuple-element.18), channel_id=1, source_target_pairs={{1,0},{2,1},{3,2},{4,3},{5,4},{6,5},{7,6},{8,7},{9,8},{10,9},{11,1... | collective-permute-start | bytes 24584 | tf_op jit(solution)/shard_map/ppermute | solution.py:23
  58.3 33.5 %collective-permute-start = (f32[64,8,4]{2,1,0:T(8,128)S(1)}, f32[64,8,4]{2,1,0:T(8,128)S(1)}, u32[]{:S(2)}, u32[]{:S(2)}) collective-permute-start(f32[64,8,4]{2,1,0:T(8,128)S(1)} %get-tuple-element.17), channel_id=1, source_target_pairs={{0,1},{1,2},{2,3},{3,4},{4,5},{5,6},{6,7},{7,8},{8,9},{9,10},{10,1... | collective-permute-start | bytes 24584 | tf_op jit(solution)/shard_map/ppermute | solution.py:22
  92.6 10.7 %collective-permute-start.3 = (f32[64,4,128]{2,1,0:T(4,128)S(1)}, f32[64,4,128]{2,1,0:T(4,128)S(1)}, u32[]{:S(2)}, u32[]{:S(2)}) collective-permute-start(f32[64,4,128]{2,1,0:T(4,128)S(1)} %get-tuple-element.16), channel_id=1, source_target_pairs={{16,0},{32,16},{48,32},{64,48},{80,64},{96,80},{112,96},{128,112},... | collective-permute-start | bytes 393224 | tf_op jit(solution)/shard_map/ppermute | solution.py:23
  100.8 15.9 %collective-permute-start.2 = (f32[64,4,128]{2,1,0:T(4,128)S(1)}, f32[64,4,128]{2,1,0:T(4,128)S(1)}, u32[]{:S(2)}, u32[]{:S(2)}) collective-permute-start(f32[64,4,128]{2,1,0:T(4,128)S(1)} %get-tuple-element.15), channel_id=1, source_target_pairs={{0,16},{16,32},{32,48},{48,64},{64,80},{80,96},{96,112},{112,128},... | collective-permute-start | bytes 393224 | tf_op jit(solution)/shard_map/ppermute | solution.py:22
  117.6 18.1 %collective-permute-start.5 = (f32[64,8,8]{2,0,1:T(8,128)S(1)}, f32[64,8,8]{2,0,1:T(8,128)S(1)}, u32[]{:S(2)}, u32[]{:S(2)}) collective-permute-start(f32[64,8,8]{2,0,1:T(8,128)S(1)} %get-tuple-element.14), channel_id=1, source_target_pairs={{1,0},{2,1},{3,2},{4,3},{5,4},{6,5},{7,6},{8,7},{9,8},{10,9},{11,1... | collective-permute-start | bytes 49160 | tf_op jit(solution)/shard_map/ppermute | solution.py:23
  119.6 24.5 %collective-permute-start.4 = (f32[64,8,8]{2,0,1:T(8,128)S(1)}, f32[64,8,8]{2,0,1:T(8,128)S(1)}, u32[]{:S(2)}, u32[]{:S(2)}) collective-permute-start(f32[64,8,8]{2,0,1:T(8,128)S(1)} %get-tuple-element.13), channel_id=1, source_target_pairs={{0,1},{1,2},{2,3},{3,4},{4,5},{5,6},{6,7},{7,8},{8,9},{9,10},{10,1... | collective-permute-start | bytes 49160 | tf_op jit(solution)/shard_map/ppermute | solution.py:22
  144.7 9.6 %collective-permute-start.7 = (f32[64,8,128]{2,0,1:T(8,128)S(1)}, f32[64,8,128]{2,0,1:T(8,128)S(1)}, u32[]{:S(2)}, u32[]{:S(2)}) collective-permute-start(f32[64,8,128]{2,0,1:T(8,128)S(1)} %convolution_select_fusion.1), channel_id=1, source_target_pairs={{16,0},{32,16},{48,32},{64,48},{80,64},{96,80},{112,96},{128,112},... | collective-permute-start | bytes 786440 | tf_op jit(solution)/shard_map/ppermute | solution.py:23
  148.1 19.1 %collective-permute-start.6 = (f32[64,8,128]{2,0,1:T(8,128)S(1)}, f32[64,8,128]{2,0,1:T(8,128)S(1)}, u32[]{:S(2)}, u32[]{:S(2)}) collective-permute-start(f32[64,8,128]{2,0,1:T(8,128)S(1)} %convolution_select_fusion.1), channel_id=1, source_target_pairs={{0,16},{16,32},{32,48},{48,64},{64,80},{80,96},{96,112},{112,128},... | collective-permute-start | bytes 786440 | tf_op jit(solution)/shard_map/ppermute | solution.py:22
where the time goes:
time: 170 us; the launch traced here: 169 us
  waiting for transfers between devices  94.5 us (56%)
  starting transfers between devices  42.7 us (25%)
  local copies, waits for them, and re-layouts  25.9 us (15%)
  matrix products  3.5 us (2%)
  other arithmetic  2.08 us (1%)
    ppermute x4, waiting for transfers between devices, with_halo(): before = lax.ppermute(last, axis, up)  64.2 us
    all_to_all x1, starting transfers between devices, body(): lax.all_to_all(velocity, 'gy', split_axis=2, concat_axis=0, tiled=True)  18 us
    unnamed x3, local copies, waits for them, and re-layouts  17.8 us
    ppermute x4, waiting for transfers between devices, with_halo(): after = lax.ppermute(first, axis, down)  17 us
    ppermute x4, starting transfers between devices, with_halo(): after = lax.ppermute(first, axis, down)  15.5 us
    all_to_all x1, waiting for transfers between devices, body(): lax.all_to_all(velocity, 'gy', split_axis=2, concat_axis=0, tiled=True)  13.4 us
    ppermute x4, starting transfers between devices, with_halo(): before = lax.ppermute(last, axis, up)  9.07 us
    all_to_all x2, local copies, waits for them, and re-layouts, body(): lax.all_to_all(velocity, 'gy', split_axis=2, concat_axis=0, tiled=True)  3.93 us
  transfers between devices with their start and end apart: 9, of which 9 were waited for; matrix products, arithmetic and copies ran while one was open for 2% of the time, Pallas kernels for 0%

commit v1 on v0

v1 whole, which is shorter than its diff:
```python
import functools

import jax
import jax.numpy as jnp
import numpy as np
from jax import lax
from jax.experimental import pallas as pl
from jax.experimental.pallas import tpu as pltpu
from jax.sharding import PartitionSpec as P

PREDICT_FIRST = -1.586134342
UPDATE_FIRST = -0.05298011854
PREDICT_SECOND = 0.8829110762
UPDATE_SECOND = 0.4435068522
SCALE_LOW = 1.149604398
SCALE_HIGH = 1.0 / 1.149604398

MESH = pl.DeviceIdType.MESH
ROWS = 8
TILE = 128
F32 = jnp.float32


def lift_matrix(extent):
    table = np.eye(extent)
    s, r = table[0::2], table[1::2]
    r = r + PREDICT_FIRST * (s + np.roll(s, -1, 0))
    s = s + UPDATE_FIRST * (r + np.roll(r, 1, 0))
    r = r + PREDICT_SECOND * (s + np.roll(s, -1, 0))
    s = s + UPDATE_SECOND * (r + np.roll(r, 1, 0))
    out = np.empty((extent, extent))
    out[0::2], out[1::2] = s * SCALE_LOW, r * SCALE_HIGH
    return out


def row_operators():
    extent, mine = 128, 64
    first = lift_matrix(extent)
    second = lift_matrix(extent // 2) @ first[0::2]
    wide = np.zeros((extent, extent))
    wide[0::2] = second

    def block(table, step):
        start = mine + ROWS * step
        return table[start : start + ROWS, mine : mine + ROWS]

    return {step: block(first, step) for step in (-1, 0, 1)}, {step: block(wide, step) for step in (-2, -1, 0, 1, 2)}


def coefficient_columns():
    first, second = row_operators()
    rows = np.arange(ROWS)
    columns, names = [], {}

    def add(name, column):
        if np.any(column != 0):
            names[name] = len(columns)
            columns.append(column)

    halo = first[1] + first[-1]
    assert not np.any((first[1] != 0) & (first[-1] != 0).any(axis=1, keepdims=True))
    for k in range(ROWS):
        source = (rows - k) % ROWS
        add(("own", k), first[0][rows, source])
        add(("halo", k), halo[rows, source])
        even = rows - rows % 2
        source = (even - k) % ROWS
        for step in (-1, 0, 1, 2):
            add((step, k), second[step][even, source])
    tail = np.zeros(ROWS)
    tail[4:] = second[-2][[4, 4, 6, 6], 0]
    add(("tail", 0), tail)
    table = np.zeros((ROWS, TILE), np.float32)
    table[:, : len(columns)] = np.stack(columns, 1)
    return table, names


COLUMNS, NAMES = coefficient_columns()


def lane_lift(value, stride):
    length = value.shape[-1]
    lane = lax.broadcasted_iota(jnp.int32, value.shape, value.ndim - 1)
    odd = (lane // stride) % 2 == 1

    def step(v, weight, mask_odd):
        near = pltpu.roll(v, stride, v.ndim - 1) + pltpu.roll(v, length - stride, v.ndim - 1)
        change = weight * near
        return v + (jnp.where(odd, change, 0.0) if mask_odd else jnp.where(odd, 0.0, change))

    value = step(value, PREDICT_FIRST, True)
    value = step(value, UPDATE_FIRST, False)
    value = step(value, PREDICT_SECOND, True)
    value = step(value, UPDATE_SECOND, False)
    return value * jnp.where(odd, SCALE_HIGH, SCALE_LOW)


def leading_lift(s, r):
    def after(a):
        return jnp.concatenate([a[1:], a[:1]], axis=0)

    def before(a):
        return jnp.concatenate([a[-1:], a[:-1]], axis=0)

    r = r + PREDICT_FIRST * (s + after(s))
    s = s + UPDATE_FIRST * (r + before(r))
    r = r + PREDICT_SECOND * (s + after(s))
    s = s + UPDATE_SECOND * (r + before(r))
    return s * SCALE_LOW, r * SCALE_HIGH


def kernel(nx, ny, v_hbm, table_hbm, out_ref, v_ref, table_ref, y_one, y_two, own, own_two, far_two, near_two, go_right,
           go_left, go_right_two, go_left_two, from_left, from_right, from_left_two, from_right_two, tail_two, send, got,
           in_sem, halo_send, halo_recv, send_sem, recv_sem):
    gx, gy = lax.axis_index("gx"), lax.axis_index("gy")
    half = (gy // 2) % 2
    blocks = ny // 4
    width = 2 * blocks * TILE

    load = pltpu.make_async_copy(v_hbm, v_ref, in_sem.at[0])
    load.start()
    load_table = pltpu.make_async_copy(table_hbm, table_ref, in_sem.at[1])
    load_table.start()

    def beside(step):
        return (lax.rem(gx + step + nx, nx), gy)

    def peer(side, j):
        block = lax.rem(gy // 4 + j // 2, blocks)
        core = lax.rem(gy + j, 2)
        return block, core, block * 4 + side * 2 + core

    barrier = pltpu.get_barrier_semaphore()
    far, near = 1 - half, half
    for step in (1, -1, 2, -2):
        pl.semaphore_signal(barrier, inc=1, device_id=beside(step), device_id_type=MESH)
    for side, first in ((far, 0), (near, 1)):
        for j in range(first, 2 * blocks):
            pl.semaphore_signal(barrier, inc=1, device_id=(gx, peer(side, j)[2]), device_id_type=MESH)

    load.wait()
    load_table.wait()

    @pl.loop(0, 4)
    def _(z):
        y_one[z] = lane_lift(v_ref[z], 1)

    @pl.loop(0, 2)
    def _(pair):
        a, b = y_one[2 * pair], y_one[2 * pair + 1]
        lane = lax.broadcasted_iota(jnp.int32, a.shape, 1)
        y_two[pair] = lane_lift(jnp.where(lane % 2 == 1, pltpu.roll(b, 1, 1), a), 2)

    row = lax.broadcasted_iota(jnp.int32, (ROWS, TILE), 0)
    low_row = row < 4
    even_row = row % 2 == 0

    def column(name):
        at = NAMES[name]
        return jnp.broadcast_to(table_ref[:, at : at + 1], (ROWS, TILE))

    def weigh(total, name, value):
        if name not in NAMES:
            return total
        term = column(name) * value
        return term if total is None else total + term

    def down(value, k):
        return value if k % ROWS == 0 else pltpu.roll(value, k % ROWS, 0)

    def x_pass(side):
        @pl.loop(0, 2 * blocks)
        def _(p):
            tile = (p // 2) * 4 + side * 2 + p % 2
            lanes = pl.ds(pl.multiple_of(tile * TILE, TILE), TILE)
            here = pl.ds(pl.multiple_of(p * TILE, TILE), TILE)
            halos = []
            for z in range(4):
                value = y_one[z, :, lanes]
                mine, halo = None, None
                for k in range(ROWS):
                    moved = down(value, k)
                    mine = weigh(mine, ("own", k), moved)
                    halo = weigh(halo, ("halo", k), moved)
                own[side, z, :, here] = mine
                halos.append(halo)
            for pair in range(2):
                a, b = halos[2 * pair], halos[2 * pair + 1]
                go_right[side, pair, :, here] = jnp.where(low_row, a, down(b, 4))
                go_left[side, pair, :, here] = jnp.where(low_row, down(a, 4), b)
            a, b = y_two[0, :, lanes], y_two[1, :, lanes]
            sums = {step: None for step in (-1, 0, 1, 2)}
            for k in range(ROWS):
                moved = jnp.where(even_row, down(a, k), down(b, k + 1))
                if k == 0:
                    near_two[side, :, here] = moved
                for step in sums:
                    sums[step] = weigh(sums[step], (step, k), moved)
            own_two[side, :, here] = sums[0]
            go_right[side, 2, :, here] = sums[1]
            go_left[side, 2, :, here] = sums[-1]
            far_two[side, :, here] = sums[2]

    wide_row = lax.broadcasted_iota(jnp.int32, (ROWS, 2 * TILE), 0)

    def pack_two(side):
        for source, target in ((far_two, go_right_two), (near_two, go_left_two)):
            packed = source[side, :, 0 : 2 * TILE]
            for block in range(1, blocks):
                value = down(source[side, :, block * 2 * TILE : (block + 1) * 2 * TILE], 2 * block)
                packed = jnp.where(wide_row // 2 == block, value, packed)
            target[side] = packed

    def halo_copies(side):
        copies = []
        for n, (source, target, step) in enumerate((
            (go_right, from_left, 1),
            (go_left, from_right, -1),
            (go_right_two, from_left_two, 2),
            (go_left_two, from_right_two, -2),
        )):
            copies.append(pltpu.make_async_remote_copy(
                src_ref=source.at[side],
                dst_ref=target.at[side],
                send_sem=halo_send.at[side, n],
                recv_sem=halo_recv.at[side, n],
                device_id=beside(step),
                device_id_type=MESH,
            ))
        return copies

    def unpack_two(side):
        tail = NAMES[("tail", 0)]
        weights = jnp.broadcast_to(table_ref[:, tail : tail + 1], (ROWS, 2 * TILE))
        for block in range(blocks):
            head = jnp.where(wide_row < 2, down(from_left_two[side], ROWS - 2 * block), 0.0)
            late = from_right_two[side]
            late = jnp.where(wide_row < 6, down(late, 4 - 2 * block), down(late, 6 - 2 * block))
            tail_two[side, :, block * 2 * TILE : (block + 1) * 2 * TILE] = head + weights * late

    def combine(side, block, core, target, slot):
        here = pl.ds(pl.multiple_of((block * 2 + core) * TILE, TILE), TILE)
        for pair in range(2):
            a, b = from_left[side, pair, :, here], from_right[side, pair, :, here]
            target[slot, 2 * pair] = own[side, 2 * pair, :, here] + jnp.where(low_row, a, down(b, 4))
            target[slot, 2 * pair + 1] = own[side, 2 * pair + 1, :, here] + jnp.where(low_row, down(a, 4), b)
        target[slot, 4] = (own_two[side, :, here] + tail_two[side, :, here]) + (
            from_left[side, 2, :, here] + from_right[side, 2, :, here])

    def tile_copy(tile):
        return pltpu.make_async_remote_copy(
            src_ref=send.at[tile],
            dst_ref=got.at[gy],
            send_sem=send_sem.at[tile],
            recv_sem=recv_sem.at[gy],
            device_id=(gx, tile),
            device_id_type=MESH,
        )

    def arrival(tile):
        return pltpu.make_async_remote_copy(
            src_ref=send.at[tile],
            dst_ref=got.at[tile],
            send_sem=send_sem.at[tile],
            recv_sem=recv_sem.at[tile],
            device_id=(gx, tile),
            device_id_type=MESH,
        )

    x_pass(far)
    pack_two(far)
    pl.semaphore_wait(barrier, 4 + 4 * blocks - 1)
    far_copies = halo_copies(far)
    for copy in far_copies:
        copy.start()
    x_pass(near)
    pack_two(near)
    near_copies = halo_copies(near)
    for copy in near_copies:
        copy.start()

    for copy in far_copies:
        copy.wait_recv()
    unpack_two(far)

    @pl.loop(0, 2 * blocks)
    def _(j):
        block, core, tile = peer(far, j)
        combine(far, block, core, send, tile)
        tile_copy(tile).start()

    for copy in near_copies:
        copy.wait_recv()
    unpack_two(near)

    @pl.loop(1, 2 * blocks)
    def _(j):
        block, core, tile = peer(near, j)
        combine(near, block, core, send, tile)
        tile_copy(tile).start()

    combine(near, gy // 4, lax.rem(gy, 2), got, gy)

    for copy in far_copies + near_copies:
        copy.wait_send()

    @pl.loop(1, 2 * blocks)
    def _(j):
        arrival(peer(near, j)[2]).wait()

    @pl.loop(0, 2 * blocks)
    def _(j):
        arrival(peer(far, j)[2]).wait()

    pairs = 2 * ny
    shape = (pairs, ROWS, TILE)
    s, r = leading_lift(got[:, 0:4:2].reshape(shape), got[:, 1:4:2].reshape(shape))
    slot = got[:, 4]
    under = pltpu.roll(slot, ROWS - 1, 1)

    def left(value):
        return pltpu.roll(value, TILE - 1, 2)

    even = jnp.stack([slot, under], axis=1).reshape(shape)
    odd = jnp.stack([left(slot), left(under)], axis=1).reshape(shape)
    coarse = leading_lift(even, odd)[0].reshape(ny, 2, ROWS, TILE)
    low, high = leading_lift(coarse[:, 0], coarse[:, 1])
    coarse = jnp.stack([low, high], axis=1).reshape(shape)
    corner = (lax.broadcasted_iota(jnp.int32, shape, 1) % 2 == 0) & (lax.broadcasted_iota(jnp.int32, shape, 2) % 2 == 0)
    out_ref[:, 0] = jnp.where(corner, coarse, s)
    out_ref[:, 1] = r


def solution(mesh):
    nx, ny = mesh.shape["gx"], mesh.shape["gy"]
    length = ny * TILE
    half = length // 2

    def body(velocity):
        out = pl.pallas_call(
            functools.partial(kernel, nx, ny),
            out_shape=jax.ShapeDtypeStruct((2 * ny, 2, ROWS, TILE), F32),
            in_specs=[pl.BlockSpec(memory_space=pl.ANY)] * 2,
            out_specs=pl.BlockSpec(memory_space=pltpu.VMEM),
            scratch_shapes=[
                pltpu.VMEM((4, ROWS, length), F32),
                pltpu.VMEM((ROWS, TILE), F32),
                pltpu.VMEM((4, ROWS, length), F32),
                pltpu.VMEM((2, ROWS, length), F32),
                pltpu.VMEM((2, 4, ROWS, half), F32),
                pltpu.VMEM((2, ROWS, half), F32),
                pltpu.VMEM((2, ROWS, half), F32),
                pltpu.VMEM((2, ROWS, half), F32),
                pltpu.VMEM((2, 3, ROWS, half), F32),
                pltpu.VMEM((2, 3, ROWS, half), F32),
                pltpu.VMEM((2, ROWS, 2 * TILE), F32),
                pltpu.VMEM((2, ROWS, 2 * TILE), F32),
                pltpu.VMEM((2, 3, ROWS, half), F32),
                pltpu.VMEM((2, 3, ROWS, half), F32),
                pltpu.VMEM((2, ROWS, 2 * TILE), F32),
                pltpu.VMEM((2, ROWS, 2 * TILE), F32),
                pltpu.VMEM((2, ROWS, half), F32),
                pltpu.VMEM((ny, 5, ROWS, TILE), F32),
                pltpu.VMEM((ny, 5, ROWS, TILE), F32),
                pltpu.SemaphoreType.DMA((2,)),
                pltpu.SemaphoreType.DMA((2, 4)),
                pltpu.SemaphoreType.DMA((2, 4)),
                pltpu.SemaphoreType.DMA((ny,)),
                pltpu.SemaphoreType.DMA((ny,)),
            ],
            compiler_params=pltpu.CompilerParams(
                collective_id=0, has_side_effects=True, vmem_limit_bytes=24 * 2**20
            ),
        )(velocity, jnp.asarray(COLUMNS))
        return out.reshape(4 * ny, ROWS, TILE)

    return jax.shard_map(
        body, mesh=mesh, in_specs=(P("gy", "gx", None),), out_specs=P(None, "gx", "gy"), check_vma=False
    )
```

time: 170 us -> 47.3 us (0.28)
  the two profiles are of different devices: /device:TPU:6 before, /device:TPU:9 now
where the time goes in v1:
time: 47.3 us; the launch traced here: 47.2 us
  Pallas kernels  44.8 us (95%)
  local copies, waits for them, and re-layouts  2.34 us (5%)
    pallas_call x1, Pallas kernels, body(): pl.pallas_call(functools.partial(kernel, nx, ny), out_shape=jax.ShapeDtyp...  44.8 us
    unnamed x5, local copies, waits for them, and re-layouts  2.34 us

profile of v1, /device:TPU:9, one launch (start us, length us, event | category | flops | bytes accessed | tf_op | source)
XLA Modules:
  0.0 47.2 jit_solution(15517345223483860083)
XLA Ops:
  0.0 0.0 copy-start
  0.0 0.9 %copy-done = f32[4,8,2048]{2,1,0:T(8,128)S(1)} copy-done((f32[4,8,2048]{2,1,0:T(8,128)S(1)}, f32[4,8,2048]{2,1,0:T(8,128)}, u32[]{:S(2)}) %copy-start) | copy-done | bytes 262168
  1.0 0.0 copy-start.1
  1.0 0.7 %copy-done.1 = f32[8,128]{1,0:T(8,128)S(1)} copy-done((f32[8,128]{1,0:T(8,128)S(1)}, f32[8,128]{1,0:T(8,128)}, u32[]{:S(2)}) %copy-start.1) | copy-done | bytes 4120
  1.6 44.8 %shard_map.28 = f32[32,2,8,128]{3,2,1,0:T(8,128)S(1)} custom-call(f32[4,8,2048]{2,1,0:T(8,128)S(1)} %copy-done, f32[8,128]{1,0:T(8,128)S(1)} %copy-done.1), custom_call_target="tpu_custom_call" | custom-call | tf_op jit(solution)/shard_map/pallas_call | solution.py:340
  46.5 0.7 %copy.4 = f32[64,8,128]{2,1,0:T(8,128)} copy(f32[64,8,128]{2,1,0:T(8,128)S(1)} %bitcast.1) | data formatting | bytes 524288
Async XLA Ops:
  0.0 0.9 %copy-start = (f32[4,8,2048]{2,1,0:T(8,128)S(1)}, f32[4,8,2048]{2,1,0:T(8,128)}, u32[]{:S(2)}) copy-start(f32[4,8,2048]{2,1,0:T(8,128)} %v_hbm.1) | copy-start | bytes 786436
  1.0 0.7 %copy-start.1 = (f32[8,128]{1,0:T(8,128)S(1)}, f32[8,128]{1,0:T(8,128)}, u32[]{:S(2)}) copy-start(f32[8,128]{1,0:T(8,128)} %constant.2.clone.table_hbm) | copy-start | bytes 12292

commit v2 on v1

v2 whole, which is shorter than its diff:
```python
import functools

import jax
import jax.numpy as jnp
import numpy as np
from jax import lax
from jax.experimental import pallas as pl
from jax.experimental.pallas import tpu as pltpu
from jax.sharding import PartitionSpec as P

PREDICT_FIRST = -1.586134342
UPDATE_FIRST = -0.05298011854
PREDICT_SECOND = 0.8829110762
UPDATE_SECOND = 0.4435068522
SCALE_LOW = 1.149604398
SCALE_HIGH = 1.0 / 1.149604398

MESH = pl.DeviceIdType.MESH
ROWS = 8
STEPS = (1, -1, 2, -2)
TILE = 128
F32 = jnp.float32


def lift_matrix(extent):
    table = np.eye(extent)
    s, r = table[0::2], table[1::2]
    r = r + PREDICT_FIRST * (s + np.roll(s, -1, 0))
    s = s + UPDATE_FIRST * (r + np.roll(r, 1, 0))
    r = r + PREDICT_SECOND * (s + np.roll(s, -1, 0))
    s = s + UPDATE_SECOND * (r + np.roll(r, 1, 0))
    out = np.empty((extent, extent))
    out[0::2], out[1::2] = s * SCALE_LOW, r * SCALE_HIGH
    return out


def row_operators():
    extent, mine = 128, 64
    first = lift_matrix(extent)
    second = lift_matrix(extent // 2) @ first[0::2]
    wide = np.zeros((extent, extent))
    wide[0::2] = second

    def block(table, step):
        start = mine + ROWS * step
        return table[start : start + ROWS, mine : mine + ROWS]

    return {step: block(first, step) for step in (-1, 0, 1)}, {step: block(wide, step) for step in (-2, -1, 0, 1, 2)}


def coefficient_columns():
    first, second = row_operators()
    columns, names = [], {}

    def add(name, column):
        if np.any(column != 0):
            names[name] = len(columns)
            columns.append(column)

    halo = first[1] + first[-1]
    assert not np.any((first[1] != 0) & (first[-1] != 0).any(axis=1, keepdims=True))
    even = np.arange(ROWS) // 2 * 2
    for j in range(ROWS):
        add(("own", j), first[0][:, j])
        add(("halo", j), halo[:, j])
        for step in (-1, 0, 1, 2):
            add((step, j), second[step][even, j])
    tail = np.zeros(ROWS)
    tail[4:] = second[-2][[4, 4, 6, 6], 0]
    add(("tail", 0), tail)
    table = np.zeros((ROWS, TILE), np.float32)
    table[:, : len(columns)] = np.stack(columns, 1)
    return table, names


COLUMNS, NAMES = coefficient_columns()


def lane_lift(s, r, stride):
    axis, length = s.ndim - 1, s.shape[-1]

    def after(a):
        return pltpu.roll(a, length - stride, axis)

    def before(a):
        return pltpu.roll(a, stride, axis)

    r = r + PREDICT_FIRST * (s + after(s))
    s = s + UPDATE_FIRST * (r + before(r))
    r = r + PREDICT_SECOND * (s + after(s))
    s = s + UPDATE_SECOND * (r + before(r))
    return s * SCALE_LOW, r * SCALE_HIGH


def swap(a, b, low, stride, axis):
    size = a.shape[axis]
    return jnp.where(low, a, pltpu.roll(b, stride, axis)), jnp.where(low, pltpu.roll(a, size - stride, axis), b)


def leading_lift(s, r):
    def after(a):
        return jnp.concatenate([a[1:], a[:1]], axis=0)

    def before(a):
        return jnp.concatenate([a[-1:], a[:-1]], axis=0)

    r = r + PREDICT_FIRST * (s + after(s))
    s = s + UPDATE_FIRST * (r + before(r))
    r = r + PREDICT_SECOND * (s + after(s))
    s = s + UPDATE_SECOND * (r + before(r))
    return s * SCALE_LOW, r * SCALE_HIGH


def kernel(nx, ny, v_hbm, table_hbm, out_ref, v_ref, table_ref, weights, y_one, y_two, own, own_two, far_two, near_two, go_right,
           go_left, go_right_two, go_left_two, from_left, from_right, from_left_two, from_right_two, tail_two, send, got,
           relay, relayed, in_sem, halo_send, halo_recv, send_sem, recv_sem, relay_send, relay_recv, go):
    gx, gy = lax.axis_index("gx"), lax.axis_index("gy")
    half = (gy // 2) % 2
    blocks = ny // 4
    width = 2 * blocks * TILE

    load = pltpu.make_async_copy(v_hbm, v_ref, in_sem.at[0])
    load.start()
    load_table = pltpu.make_async_copy(table_hbm, table_ref, in_sem.at[1])
    load_table.start()

    other = gy + 2 - 4 * half

    def wraps(step):
        return jnp.logical_or(gx + step < 0, gx + step >= nx)

    def beside(step):
        return (lax.rem(gx + step + nx, nx), gy)

    def nearest(step):
        return (lax.rem(gx + step + nx, nx), jnp.where(wraps(step), other, gy))

    def peer(side, j):
        block = lax.rem(gy // 4 + j // 2, blocks)
        core = lax.rem(gy + j, 2)
        return block, core, block * 4 + side * 2 + core

    barrier = pltpu.get_barrier_semaphore()
    far, near = 1 - half, half
    for step in STEPS:
        pl.semaphore_signal(barrier, inc=1, device_id=nearest(step), device_id_type=MESH)
    for j in range(1, 2 * blocks):
        pl.semaphore_signal(barrier, inc=1, device_id=(gx, peer(near, j)[2]), device_id_type=MESH)

    def greet_far(semaphore):
        for j in range(2 * blocks):
            pl.semaphore_signal(semaphore, inc=1, device_id=(gx, peer(far, j)[2]), device_id_type=MESH)

    for n in (0, 2):
        @pl.when(wraps(-STEPS[n]))
        def _():
            pl.semaphore_signal(barrier, inc=1, device_id=beside(-STEPS[n]), device_id_type=MESH)

    @pl.when(half == 0)
    def _():
        greet_far(barrier)

    load_table.wait()
    for at in range(len(NAMES)):
        weights[at] = jnp.broadcast_to(table_ref[:, at : at + 1], (ROWS, TILE))
    load.wait()

    lane = lax.broadcasted_iota(jnp.int32, (ROWS, TILE), 1)
    row = lax.broadcasted_iota(jnp.int32, (ROWS, TILE), 0)
    low_row = row < 4
    even_row = row % 2 == 0

    def low_lanes(stride):
        return jnp.concatenate([(lane // stride) % 2] * ny, axis=1) == 0

    lows = []
    for pair in range(2):
        s, r = swap(v_ref[2 * pair], v_ref[2 * pair + 1], low_lanes(1), 1, 1)
        s, r = lane_lift(s, r, 2)
        y_one[2 * pair] = s
        y_one[2 * pair + 1] = r
        lows.append(s)
    s, r = lane_lift(*swap(*lows, low_lanes(2), 2, 1), 4)
    y_two[0], y_two[1] = swap(s, r, low_lanes(2), 2, 1)

    def weigh(total, name, value):
        if name not in NAMES:
            return total
        term = weights[NAMES[name]] * value
        return term if total is None else total + term

    def down(value, k):
        return value if k % ROWS == 0 or isinstance(value, float) else pltpu.roll(value, k % ROWS, 0)

    def x_pass(side):
        @pl.loop(0, 2 * blocks)
        def _(p):
            tile = (p // 2) * 4 + side * 2 + p % 2
            lanes = pl.ds(pl.multiple_of(tile * TILE, TILE), TILE)
            here = pl.ds(pl.multiple_of(p * TILE, TILE), TILE)

            def spread(ref, z, j):
                return jnp.broadcast_to(ref[z, j : j + 1, lanes], (ROWS, TILE))

            mine, halos = [None] * 4, [None] * 4
            for j in range(ROWS):
                for z in range(4):
                    value = spread(y_one, z, j)
                    mine[z] = weigh(mine[z], ("own", j), value)
                    halos[z] = weigh(halos[z], ("halo", j), value)
            for z in range(4):
                own[side, z, :, here] = mine[z]
            for pair in range(2):
                a, b = halos[2 * pair], halos[2 * pair + 1]
                go_right[side, pair, :, here] = jnp.where(low_row, a, down(b, 4))
                go_left[side, pair, :, here] = jnp.where(low_row, down(a, 4), b)
            sums = {step: None for step in (-1, 0, 1, 2)}
            for j in range(ROWS):
                value = jnp.where(even_row, spread(y_two, 0, j), spread(y_two, 1, j))
                if j == 0:
                    near_two[side, :, here] = value
                for step in sums:
                    sums[step] = weigh(sums[step], (step, j), value)
            own_two[side, :, here] = sums[0]
            go_right[side, 2, :, here] = sums[1]
            go_left[side, 2, :, here] = sums[-1]
            far_two[side, :, here] = sums[2]

    wide_row = lax.broadcasted_iota(jnp.int32, (ROWS, 2 * TILE), 0)

    def pack_two(side):
        for source, target in ((far_two, go_right_two), (near_two, go_left_two)):
            packed = source[side, :, 0 : 2 * TILE]
            for block in range(1, blocks):
                value = down(source[side, :, block * 2 * TILE : (block + 1) * 2 * TILE], 2 * block)
                packed = jnp.where(wide_row // 2 == block, value, packed)
            target[side] = packed

    messages = (
        (go_right, from_left),
        (go_left, from_right),
        (go_right_two, from_left_two),
        (go_left_two, from_right_two),
    )

    def halo_copy(n, side, slot, device):
        return pltpu.make_async_remote_copy(
            src_ref=messages[n][0].at[side],
            dst_ref=messages[n][1].at[slot],
            send_sem=halo_send.at[side, n],
            recv_sem=halo_recv.at[slot, n],
            device_id=device,
            device_id_type=MESH,
        )

    def halo_out(n, side):
        step = STEPS[n]
        if side is near and step > 0:
            return halo_copy(n, side, side, beside(step))
        return halo_copy(n, side, side + jnp.where(wraps(step), 2, 0), nearest(step))

    def halo_in(n, side, wrapped):
        return halo_copy(n, side, side + (2 if wrapped else 0), beside(STEPS[n]))

    came = [wraps(-step) for step in STEPS]
    straight = [jnp.logical_not(flag) for flag in came]

    def kept(side):
        return straight if side is far else [gx >= 0, straight[1], gx >= 0, straight[3]]

    def only(flag, value):
        if isinstance(flag, bool):
            return value if flag else 0.0
        return jnp.where(flag, value, 0.0)

    def unpack_two(slot, keep):
        tail = NAMES[("tail", 0)]
        tails = jnp.broadcast_to(table_ref[:, tail : tail + 1], (ROWS, 2 * TILE))
        for block in range(blocks):
            head = jnp.where(wide_row < 2, down(from_left_two[slot], ROWS - 2 * block), 0.0)
            late = from_right_two[slot]
            late = jnp.where(wide_row < 6, down(late, 4 - 2 * block), down(late, 6 - 2 * block))
            tail_two[slot, :, block * 2 * TILE : (block + 1) * 2 * TILE] = only(keep[2], head) + only(keep[3], tails * late)

    def spread_rows(a, b):
        return [jnp.where(low_row, a, down(b, 4)), jnp.where(low_row, down(a, 4), b)]

    def halo_tiles(slot, keep, here):
        tiles = []
        for pair in range(2):
            tiles += spread_rows(only(keep[0], from_left[slot, pair, :, here]), only(keep[1], from_right[slot, pair, :, here]))
        a, b = only(keep[0], from_left[slot, 2, :, here]), only(keep[1], from_right[slot, 2, :, here])
        return tiles + [tail_two[slot, :, here] + (a + b)]

    def lanes_of(block, core):
        return pl.ds(pl.multiple_of((block * 2 + core) * TILE, TILE), TILE)

    def combine(side, block, core, target, slot):
        here = lanes_of(block, core)
        tiles = halo_tiles(side, kept(side), here)
        for n in range(4):
            target[slot, n] = own[side, n, :, here] + tiles[n]
        target[slot, 4] = own_two[side, :, here] + tiles[4]

    def tile_copy(tile):
        return pltpu.make_async_remote_copy(
            src_ref=send.at[tile],
            dst_ref=got.at[gy],
            send_sem=send_sem.at[tile],
            recv_sem=recv_sem.at[gy],
            device_id=(gx, tile),
            device_id_type=MESH,
        )

    def arrival(tile):
        return pltpu.make_async_remote_copy(
            src_ref=send.at[tile],
            dst_ref=got.at[tile],
            send_sem=send_sem.at[tile],
            recv_sem=recv_sem.at[tile],
            device_id=(gx, tile),
            device_id_type=MESH,
        )

    x_pass(far)
    pack_two(far)
    late_greetings = jnp.where(wraps(1), 2, jnp.where(wraps(2), 1, 0))
    pl.semaphore_wait(barrier, 4 + 2 * blocks - 1 + 2 * blocks * half + late_greetings)
    for n in range(4):
        halo_out(n, far).start()

    @pl.when(half == 1)
    def _():
        greet_far(go)

    x_pass(near)
    pack_two(near)
    for n in range(4):
        halo_out(n, near).start()

    def await_halos(side):
        for n in range(4):
            @pl.when(kept(side)[n])
            def _():
                halo_in(n, side, False).wait_recv()
        unpack_two(side, kept(side))

    def relay_copy(slot, tile, count):
        return pltpu.make_async_remote_copy(
            src_ref=relay.at[tile, pl.ds(0, count)],
            dst_ref=relayed.at[slot, pl.ds(0, count)],
            send_sem=relay_send.at[tile],
            recv_sem=relay_recv.at[slot],
            device_id=(gx, tile),
            device_id_type=MESH,
        )

    def at_ends(act, *ends):
        for low in ends:
            for place, count in ((0, 3), (1, 1)):
                @pl.when(gx == (place if low else nx - 1 - place))
                def _():
                    act(low, count)

    def pass_on(side, low, count):
        first = 1 if side is near else 0
        ones, twos = (from_left, 2) if low else (from_right, 3)
        slot = 2 + side

        def fill(block, core, target, place):
            here = lanes_of(block, core)
            value = tail_two[slot, :, here]
            if count == 3:
                target[place, 0] = value + ones[slot, 2, :, here]
                for pair in range(2):
                    target[place, 1 + pair] = ones[slot, pair, :, here]
            else:
                target[place, 0] = value

        for n in ((twos - 2, twos) if count == 3 else (twos,)):
            halo_in(n, side, True).wait_recv()
        unpack_two(slot, [None, None, low, not low])

        @pl.loop(first, 2 * blocks)
        def _(j):
            block, core, tile = peer(side, j)
            fill(block, core, relay, tile)
            relay_copy(gy, tile, count).start()

        if first:
            fill(gy // 4, lax.rem(gy, 2), relayed, gy)

    await_halos(far)

    @pl.loop(0, 2 * blocks)
    def _(j):
        block, core, tile = peer(far, j)
        combine(far, block, core, send, tile)

        @pl.when(half == 1)
        def _():
            tile_copy(tile).start()

    @pl.when(half == 1)
    def _():
        at_ends(functools.partial(pass_on, far), False)

    await_halos(near)

    @pl.loop(1, 2 * blocks)
    def _(j):
        block, core, tile = peer(near, j)
        combine(near, block, core, send, tile)
        tile_copy(tile).start()

    combine(near, gy // 4, lax.rem(gy, 2), got, gy)

    @pl.when(half == 0)
    def _():
        pl.semaphore_wait(go, 2 * blocks)

        @pl.loop(0, 2 * blocks)
        def _(j):
            tile_copy(peer(far, j)[2]).start()

        at_ends(functools.partial(pass_on, far), False)

    at_ends(functools.partial(pass_on, near), True, False)

    for n in range(4):
        halo_out(n, far).wait_send()
        halo_out(n, near).wait_send()

    @pl.loop(1, 2 * blocks)
    def _(j):
        arrival(peer(near, j)[2]).wait()

    @pl.loop(0, 2 * blocks)
    def _(j):
        arrival(peer(far, j)[2]).wait()

    def take_over(low, count):
        for side, first in ((near, 1),) if low else ((near, 1), (far, 0)):
            @pl.loop(first, 2 * blocks)
            def _(j):
                tile = peer(side, j)[2]
                relay_copy(tile, tile, count).wait()

        for side, back in ((near, far),) if low else ((near, far), (far, near)):
            @pl.loop(0, 2 * blocks)
            def _(j):
                tile, owner = peer(side, j)[2], peer(back, j)[2]
                if count == 3:
                    for pair in range(2):
                        value = relayed[tile, 1 + pair]
                        for n, rows in enumerate(spread_rows(value, 0.0) if low else spread_rows(0.0, value)):
                            got[owner, 2 * pair + n] += rows
                got[owner, 4] += relayed[tile, 0]

    at_ends(take_over, True, False)

    pairs = 2 * ny
    shape = (pairs, ROWS, TILE)
    wide = lax.broadcasted_iota(jnp.int32, (ny, ROWS, TILE), 2) % 2 == 0
    pairs_one = [swap(got[:, n], got[:, n + 1], wide, 1, 2) for n in (0, 2)]
    s, r = leading_lift(*(jnp.stack(both, axis=1).reshape(shape) for both in zip(*pairs_one)))
    slot = got[:, 4]
    under = pltpu.roll(slot, ROWS - 1, 1)

    def left(value):
        return pltpu.roll(value, TILE - 1, 2)

    even = jnp.stack([slot, under], axis=1).reshape(shape)
    odd = jnp.stack([left(slot), left(under)], axis=1).reshape(shape)
    coarse = leading_lift(even, odd)[0].reshape(ny, 2, ROWS, TILE)
    low, high = leading_lift(coarse[:, 0], coarse[:, 1])
    coarse = jnp.stack([low, high], axis=1).reshape(shape)
    corner = (lax.broadcasted_iota(jnp.int32, shape, 1) % 2 == 0) & (lax.broadcasted_iota(jnp.int32, shape, 2) % 2 == 0)
    out_ref[:, 0] = jnp.where(corner, coarse, s)
    out_ref[:, 1] = r


def solution(mesh):
    nx, ny = mesh.shape["gx"], mesh.shape["gy"]
    length = ny * TILE
    half = length // 2

    def body(velocity):
        out = pl.pallas_call(
            functools.partial(kernel, nx, ny),
            out_shape=jax.ShapeDtypeStruct((2 * ny, 2, ROWS, TILE), F32),
            in_specs=[pl.BlockSpec(memory_space=pl.ANY)] * 2,
            out_specs=pl.BlockSpec(memory_space=pltpu.VMEM),
            scratch_shapes=[
                pltpu.VMEM((4, ROWS, length), F32),
                pltpu.VMEM((ROWS, TILE), F32),
                pltpu.VMEM((len(NAMES), ROWS, TILE), F32),
                pltpu.VMEM((4, ROWS, length), F32),
                pltpu.VMEM((2, ROWS, length), F32),
                pltpu.VMEM((2, 4, ROWS, half), F32),
                pltpu.VMEM((2, ROWS, half), F32),
                pltpu.VMEM((2, ROWS, half), F32),
                pltpu.VMEM((2, ROWS, half), F32),
                pltpu.VMEM((2, 3, ROWS, half), F32),
                pltpu.VMEM((2, 3, ROWS, half), F32),
                pltpu.VMEM((2, ROWS, 2 * TILE), F32),
                pltpu.VMEM((2, ROWS, 2 * TILE), F32),
                pltpu.VMEM((4, 3, ROWS, half), F32),
                pltpu.VMEM((4, 3, ROWS, half), F32),
                pltpu.VMEM((4, ROWS, 2 * TILE), F32),
                pltpu.VMEM((4, ROWS, 2 * TILE), F32),
                pltpu.VMEM((4, ROWS, half), F32),
                pltpu.VMEM((ny, 5, ROWS, TILE), F32),
                pltpu.VMEM((ny, 5, ROWS, TILE), F32),
                pltpu.VMEM((ny, 3, ROWS, TILE), F32),
                pltpu.VMEM((ny, 3, ROWS, TILE), F32),
                pltpu.SemaphoreType.DMA((2,)),
                pltpu.SemaphoreType.DMA((2, 4)),
                pltpu.SemaphoreType.DMA((4, 4)),
                pltpu.SemaphoreType.DMA((ny,)),
                pltpu.SemaphoreType.DMA((ny,)),
                pltpu.SemaphoreType.DMA((ny,)),
                pltpu.SemaphoreType.DMA((ny,)),
                pltpu.SemaphoreType.REGULAR,
            ],
            compiler_params=pltpu.CompilerParams(collective_id=0, has_side_effects=True),
        )(velocity, jnp.asarray(COLUMNS))
        return out.reshape(4 * ny, ROWS, TILE)

    return jax.shard_map(
        body, mesh=mesh, in_specs=(P("gy", "gx", None),), out_specs=P(None, "gx", "gy"), check_vma=False
    )
```

time: 47.3 us -> 39.9 us (0.84)
  the two profiles are of different devices: /device:TPU:9 before, /device:TPU:505 now
where the time goes in v2:
time: 39.9 us; the launch traced here: 39.3 us
  Pallas kernels  37.7 us (94%)
  local copies, waits for them, and re-layouts  1.67 us (4%)
    pallas_call x1, Pallas kernels, body(): pl.pallas_call(functools.partial(kernel, nx, ny), out_shape=jax.ShapeDtyp...  37.7 us
    unnamed x1, local copies, waits for them, and re-layouts  1.67 us

profile of v2, /device:TPU:505, one launch (start us, length us, event | category | flops | bytes accessed | tf_op | source)
XLA Modules:
  0.0 39.3 jit_solution(2347423966356674771)
XLA Ops:
  0.0 37.7 %shard_map.28 = f32[32,2,8,128]{3,2,1,0:T(8,128)} custom-call(f32[4,8,2048]{2,1,0:T(8,128)} %v_hbm.1, f32[8,128]{1,0:T(8,128)} %constant.2.clone.table_hbm), custom_call_target="tpu_custom_call" | custom-call | tf_op jit(solution)/shard_map/pallas_call | solution.py:489
  37.7 1.7 %copy.4 = f32[64,8,128]{2,1,0:T(8,128)} copy(f32[64,8,128]{2,1,0:T(8,128)} %bitcast.1) | data formatting | bytes 524288

commit v3 on v2

--- a/solution.py
+++ b/solution.py
@@ -32,6 +32,10 @@
     out = np.empty((extent, extent))
     out[0::2], out[1::2] = s * SCALE_LOW, r * SCALE_HIGH
     return out
+
+
+LOW_TAPS = [float(tap) for tap in lift_matrix(32)[16, 16:21]]
+HIGH_TAPS = [float(tap) for tap in lift_matrix(32)[17, 17:21]]
 
 
 def row_operators():
@@ -79,11 +83,29 @@
 def lane_lift(s, r, stride):
     axis, length = s.ndim - 1, s.shape[-1]
 
+    def at(a, pairs):
+        return pltpu.roll(a, (-pairs * stride) % length, axis) if pairs else a
+
+    low, high = LOW_TAPS, HIGH_TAPS
+    s_next, s_last, r_next, r_last = at(s, 1), at(s, -1), at(r, 1), at(r, -1)
+    s_after, s_before, r_before = at(s, 2), at(s, -2), at(r, -2)
+    s_out = (low[0] * s + low[2] * (s_next + s_last)) + low[4] * (s_after + s_before)
+    s_out = s_out + (low[1] * (r + r_last) + low[3] * (r_next + r_before))
+    r_out = (high[0] * r + high[2] * (r_next + r_last)) + (high[1] * (s + s_next) + high[3] * (s_last + s_after))
+    return s_out, r_out
+
+
+def swap(a, b, low, stride, axis):
+    size = a.shape[axis]
+    return jnp.where(low, a, pltpu.roll(b, stride, axis)), jnp.where(low, pltpu.roll(a, size - stride, axis), b)
+
+
+def leading_lift(s, r):
     def after(a):
-        return pltpu.roll(a, length - stride, axis)
+        return jnp.concatenate([a[1:], a[:1]], axis=0)
 
     def before(a):
-        return pltpu.roll(a, stride, axis)
+        return jnp.concatenate([a[-1:], a[:-1]], axis=0)
 
     r = r + PREDICT_FIRST * (s + after(s))
     s = s + UPDATE_FIRST * (r + before(r))
@@ -92,28 +114,9 @@
     return s * SCALE_LOW, r * SCALE_HIGH
 
 
-def swap(a, b, low, stride, axis):
-    size = a.shape[axis]
-    return jnp.where(low, a, pltpu.roll(b, stride, axis)), jnp.where(low, pltpu.roll(a, size - stride, axis), b)
-
-
-def leading_lift(s, r):
-    def after(a):
-        return jnp.concatenate([a[1:], a[:1]], axis=0)
-
-    def before(a):
-        return jnp.concatenate([a[-1:], a[:-1]], axis=0)
-
-    r = r + PREDICT_FIRST * (s + after(s))
-    s = s + UPDATE_FIRST * (r + before(r))
-    r = r + PREDICT_SECOND * (s + after(s))
-    s = s + UPDATE_SECOND * (r + before(r))
-    return s * SCALE_LOW, r * SCALE_HIGH
-
-
 def kernel(nx, ny, v_hbm, table_hbm, out_ref, v_ref, table_ref, weights, y_one, y_two, own, own_two, far_two, near_two, go_right,
            go_left, go_right_two, go_left_two, from_left, from_right, from_left_two, from_right_two, tail_two, send, got,
-           relay, relayed, in_sem, halo_send, halo_recv, send_sem, recv_sem, relay_send, relay_recv, go):
+           relay, relayed, in_sem, halo_send, halo_recv, send_sem, recv_sem, relay_send, relay_recv, go, ready, join):
     gx, gy = lax.axis_index("gx"), lax.axis_index("gy")
     half = (gy // 2) % 2
     blocks = ny // 4
@@ -142,17 +145,34 @@
 
     barrier = pltpu.get_barrier_semaphore()
     far, near = 1 - half, half
-    for step in STEPS:
-        pl.semaphore_signal(barrier, inc=1, device_id=nearest(step), device_id_type=MESH)
-    for j in range(1, 2 * blocks):
-        pl.semaphore_signal(barrier, inc=1, device_id=(gx, peer(near, j)[2]), device_id_type=MESH)
+    answered = [wraps(step) & (half == 0) if step > 0 else gx < 0 for step in STEPS]
+    answers = [wraps(-step) & (half == 1) if step > 0 else gx < 0 for step in STEPS]
+    for n in range(4):
+        back = (1, 0, 3, 2)[n]
+
+        @pl.when(jnp.logical_not(answers[back]))
+        def _():
+            pl.semaphore_signal(barrier, inc=1, device_id=nearest(STEPS[n]), device_id_type=MESH)
+    column = gy // 4
+    pl.semaphore_signal(barrier, inc=1, device_id=(gx, peer(near, 1)[2]), device_id_type=MESH)
+
+    def signal_blocks(semaphore, flag):
+        for block in range(blocks):
+            @pl.when(flag(block))
+            def _():
+                for core in range(2):
+                    tile = block * 4 + near * 2 + core
+                    pl.semaphore_signal(semaphore, inc=1, device_id=(gx, tile), device_id_type=MESH)
+
+    signal_blocks(barrier, lambda block: column < block)
 
     def greet_far(semaphore):
         for j in range(2 * blocks):
             pl.semaphore_signal(semaphore, inc=1, device_id=(gx, peer(far, j)[2]), device_id_type=MESH)
 
-    for n in (0, 2):
-        @pl.when(wraps(-STEPS[n]))
+    heard = (half == 0)
+    for n in range(4):
+        @pl.when(wraps(-STEPS[n]) & (heard if STEPS[n] < 0 else gx >= 0))
         def _():
             pl.semaphore_signal(barrier, inc=1, device_id=beside(-STEPS[n]), device_id_type=MESH)
 
@@ -243,30 +263,44 @@
         (go_left_two, from_right_two),
     )
 
-    def halo_copy(n, side, slot, device):
+    def halo_copy(n, side, slot, device, block=None):
+        source, target = messages[n][0].at[side], messages[n][1].at[slot]
+        at = n
+        if block is not None:
+            lanes = pl.ds(pl.multiple_of(block * 2 * TILE, 2 * TILE), 2 * TILE)
+            source, target = source.at[:, :, lanes], target.at[:, :, lanes]
+            at = 4 + n * blocks + block
         return pltpu.make_async_remote_copy(
-            src_ref=messages[n][0].at[side],
-            dst_ref=messages[n][1].at[slot],
-            send_sem=halo_send.at[side, n],
-            recv_sem=halo_recv.at[slot, n],
+            src_ref=source,
+            dst_ref=target,
+            send_sem=halo_send.at[side, at],
+            recv_sem=halo_recv.at[slot, at],
             device_id=device,
             device_id_type=MESH,
         )
 
-    def halo_out(n, side):
+    def halo_out(n, side, block=None):
         step = STEPS[n]
-        if side is near and step > 0:
-            return halo_copy(n, side, side, beside(step))
-        return halo_copy(n, side, side + jnp.where(wraps(step), 2, 0), nearest(step))
-
-    def halo_in(n, side, wrapped):
-        return halo_copy(n, side, side + (2 if wrapped else 0), beside(STEPS[n]))
+        if side is near:
+            by_other = wraps(step) & (half == 1) & (step < 0)
+            gx_to, gy_to = beside(step)
+            return halo_copy(n, side, jnp.where(by_other, 3, side), (gx_to, jnp.where(by_other, other, gy_to)), block)
+        return halo_copy(n, side, jnp.where(wraps(step), 2, side), nearest(step), block)
+
+    def halo_in(n, side, block=None):
+        return halo_copy(n, side, side, beside(STEPS[n]), block)
+
+    def wrapped_in(n, side, block=None):
+        return halo_copy(n, side, 2 if side is near else 3, beside(STEPS[n]), block)
+
+    def block_from_here(i):
+        return lax.rem(gy // 4 + i, blocks)
 
     came = [wraps(-step) for step in STEPS]
     straight = [jnp.logical_not(flag) for flag in came]
 
     def kept(side):
-        return straight if side is far else [gx >= 0, straight[1], gx >= 0, straight[3]]
+        return straight if side is far else [True, straight[1] | (half == 0), True, straight[3] | (half == 0)]
 
     def only(flag, value):
         if isinstance(flag, bool):
@@ -324,26 +358,70 @@
 
     x_pass(far)
     pack_two(far)
-    late_greetings = jnp.where(wraps(1), 2, jnp.where(wraps(2), 1, 0))
-    pl.semaphore_wait(barrier, 4 + 2 * blocks - 1 + 2 * blocks * half + late_greetings)
-    for n in range(4):
-        halo_out(n, far).start()
+    late_greetings = jnp.where(wraps(1), 2, jnp.where(wraps(2), 1, 0)) * half
+    late_greetings += jnp.where(wraps(-1), 2, jnp.where(wraps(-2), 1, 0)) * jnp.where(heard, 1, 0)
+    near_first = (half == 0) | wraps(8)
+
+    @pl.when(near_first)
+    def _():
+        x_pass(near)
+        pack_two(near)
+
+    pl.semaphore_wait(barrier, 5 + 2 * column + 2 * blocks * half + late_greetings)
 
     @pl.when(half == 1)
     def _():
-        greet_far(go)
-
-    x_pass(near)
-    pack_two(near)
+        greet_far(go.at[column])
+
+    def send_far_halos(n, condition):
+        @pl.when(condition)
+        def _():
+            if n > 1:
+                halo_out(n, far).start()
+            else:
+                @pl.loop(0, blocks)
+                def _(i):
+                    halo_out(n, far, block_from_here(i)).start()
+
+    around = [wraps(step) & (heard if step < 0 else gx >= 0) for step in STEPS]
+    for n in (2, 0):
+        send_far_halos(n, around[n] & jnp.logical_not(answered[n]))
     for n in range(4):
-        halo_out(n, near).start()
-
-    def await_halos(side):
+        @pl.when(around[n])
+        def _():
+            halo_out(n, near).start()
+    for n in (2, 3, 0, 1):
+        send_far_halos(n, jnp.logical_not(around[n]) if STEPS[n] > 0 else gx >= 0)
+
+    @pl.when(half == 1)
+    def _():
+        for n in (0, 2):
+            @pl.when(answers[n])
+            def _():
+                pl.semaphore_signal(ready.at[n], inc=1, device_id=nearest(-STEPS[n]), device_id_type=MESH)
+
+    signal_blocks(join, lambda block: column > block)
+
+    @pl.when(jnp.logical_not(near_first))
+    def _():
+        x_pass(near)
+        pack_two(near)
+
+    late_near = (half == 1) & (lax.rem(gx, 4) == 0) & (gx < 24)
+
+    def send_near_halos(flag):
         for n in range(4):
+            @pl.when(flag & (jnp.logical_not(wraps(STEPS[n])) | ((half == 1) & (STEPS[n] < 0))))
+            def _():
+                halo_out(n, near).start()
+
+    send_near_halos(jnp.logical_not(late_near) | wraps(-2))
+
+    def await_halos(numbers, side, block=None):
+        for n in numbers:
             @pl.when(kept(side)[n])
             def _():
-                halo_in(n, side, False).wait_recv()
-        unpack_two(side, kept(side))
+                halo_in(n, side, block).wait_recv()
 
     def relay_copy(slot, tile, count):
         return pltpu.make_async_remote_copy(
@@ -363,9 +441,8 @@
                     act(low, count)
 
     def pass_on(side, low, count):
-        first = 1 if side is near else 0
         ones, twos = (from_left, 2) if low else (from_right, 3)
-        slot = 2 + side
+        slot = 2 if side is near else 3
 
         def fill(block, core, target, place):
             here = lanes_of(block, core)
@@ -377,35 +454,60 @@
             else:
                 target[place, 0] = value
 
-        for n in ((twos - 2, twos) if count == 3 else (twos,)):
-            halo_in(n, side, True).wait_recv()
+        wrapped_in(twos, side).wait_recv()
+        if count == 3 and side is far:
+            wrapped_in(twos - 2, side).wait_recv()
+        elif count == 3:
+            for block in range(blocks):
+                wrapped_in(twos - 2, side, block).wait_recv()
         unpack_two(slot, [None, None, low, not low])
 
-        @pl.loop(first, 2 * blocks)
+        @pl.loop(1 if side is near else 0, 2 * blocks)
         def _(j):
             block, core, tile = peer(side, j)
             fill(block, core, relay, tile)
             relay_copy(gy, tile, count).start()
 
-        if first:
+        if side is near:
             fill(gy // 4, lax.rem(gy, 2), relayed, gy)
 
-    await_halos(far)
-
-    @pl.loop(0, 2 * blocks)
-    def _(j):
-        block, core, tile = peer(far, j)
-        combine(far, block, core, send, tile)
-
-        @pl.when(half == 1)
+    await_halos((2, 3), far)
+    unpack_two(far, kept(far))
+
+    @pl.loop(0, blocks)
+    def _(i):
+        await_halos((0, 1), far, block_from_here(i))
+        for j in range(2):
+            block, core, tile = peer(far, 2 * i + j)
+            combine(far, block, core, send, tile)
+
+            @pl.when(half == 1)
+            def _():
+                tile_copy(tile).start()
+
+    send_near_halos(late_near & jnp.logical_not(wraps(-2)))
+
+    for n in (0, 2):
+        @pl.when(answered[n])
         def _():
-            tile_copy(tile).start()
-
-    @pl.when(half == 1)
+            pl.semaphore_wait(ready.at[n], 1)
+        send_far_halos(n, answered[n])
+
+    @pl.when(half == 0)
     def _():
+        @pl.loop(0, blocks)
+        def _(block):
+            pl.semaphore_wait(go.at[block], 2)
+            for core in range(2):
+                tile_copy(block * 4 + far * 2 + core).start()
+
         at_ends(functools.partial(pass_on, far), False)
 
-    await_halos(near)
+    await_halos(range(4), near)
+    unpack_two(near, kept(near))
+    @pl.when(column < blocks - 1)
+    def _():
+        pl.semaphore_wait(join, 2 * (blocks - 1 - column))
 
     @pl.loop(1, 2 * blocks)
     def _(j):
@@ -415,38 +517,24 @@
 
     combine(near, gy // 4, lax.rem(gy, 2), got, gy)
 
-    @pl.when(half == 0)
-    def _():
-        pl.semaphore_wait(go, 2 * blocks)
-
-        @pl.loop(0, 2 * blocks)
-        def _(j):
-            tile_copy(peer(far, j)[2]).start()
-
-        at_ends(functools.partial(pass_on, far), False)
-
     at_ends(functools.partial(pass_on, near), True, False)
 
-    for n in range(4):
-        halo_out(n, far).wait_send()
-        halo_out(n, near).wait_send()
 
     @pl.loop(1, 2 * blocks)
     def _(j):
-        arrival(peer(near, j)[2]).wait()
+        arrival(peer(near, j)[2]).wait_recv()
 
     @pl.loop(0, 2 * blocks)
     def _(j):
-        arrival(peer(far, j)[2]).wait()
+        arrival(peer(far, j)[2]).wait_recv()
 
     def take_over(low, count):
-        for side, first in ((near, 1),) if low else ((near, 1), (far, 0)):
+        def take(side, first, back):
             @pl.loop(first, 2 * blocks)
             def _(j):
                 tile = peer(side, j)[2]
-                relay_copy(tile, tile, count).wait()
-
-        for side, back in ((near, far),) if low else ((near, far), (far, near)):
+                relay_copy(tile, tile, count).wait_recv()
+
             @pl.loop(0, 2 * blocks)
             def _(j):
                 tile, owner = peer(side, j)[2], peer(back, j)[2]
@@ -457,6 +545,12 @@
                             got[owner, 2 * pair + n] += rows
                 got[owner, 4] += relayed[tile, 0]
 
+        take(near, 1, far)
+        if not low:
+            @pl.when(half == 1)
+            def _():
+                take(far, 0, near)
+
     at_ends(take_over, True, False)
 
     pairs = 2 * ny
@@ -478,6 +572,38 @@
     corner = (lax.broadcasted_iota(jnp.int32, shape, 1) % 2 == 0) & (lax.broadcasted_iota(jnp.int32, shape, 2) % 2 == 0)
     out_ref[:, 0] = jnp.where(corner, coarse, s)
     out_ref[:, 1] = r
+
+    for n in range(4):
+        halo_out(n, near).wait_send()
+    for n in (2, 3):
+        halo_out(n, far).wait_send()
+
+    @pl.loop(0, blocks)
+    def _(i):
+        for n in (0, 1):
+            halo_out(n, far, block_from_here(i)).wait_send()
+
+    @pl.loop(1, 2 * blocks)
+    def _(j):
+        tile_copy(peer(near, j)[2]).wait_send()
+
+    @pl.loop(0, 2 * blocks)
+    def _(j):
+        tile_copy(peer(far, j)[2]).wait_send()
+
+    def drain(low, count):
+        @pl.loop(1, 2 * blocks)
+        def _(j):
+            relay_copy(gy, peer(near, j)[2], count).wait_send()
+
+        if not low:
+            @pl.when(half == 0)
+            def _():
+                @pl.loop(0, 2 * blocks)
+                def _(j):
+                    relay_copy(gy, peer(far, j)[2], count).wait_send()
+
+    at_ends(drain, True, False)
 
 
 def solution(mesh):
@@ -515,12 +641,14 @@
                 pltpu.VMEM((ny, 3, ROWS, TILE), F32),
                 pltpu.VMEM((ny, 3, ROWS, TILE), F32),
                 pltpu.SemaphoreType.DMA((2,)),
-                pltpu.SemaphoreType.DMA((2, 4)),
-                pltpu.SemaphoreType.DMA((4, 4)),
+                pltpu.SemaphoreType.DMA((2, 4 + ny // 2)),
+                pltpu.SemaphoreType.DMA((4, 4 + ny // 2)),
                 pltpu.SemaphoreType.DMA((ny,)),
                 pltpu.SemaphoreType.DMA((ny,)),
                 pltpu.SemaphoreType.DMA((ny,)),
                 pltpu.SemaphoreType.DMA((ny,)),
+                pltpu.SemaphoreType.REGULAR((ny // 4,)),
+                pltpu.SemaphoreType.REGULAR((4,)),
                 pltpu.SemaphoreType.REGULAR,
             ],
             compiler_params=pltpu.CompilerParams(collective_id=0, has_side_effects=True),

time: 39.9 us -> 39 us (0.977)
  Pallas kernels: 37.7 us -> 37.1 us
    pallas_call x1, Pallas kernels: 37.7 us -> 37.1 us  [body(): pl.pallas_call(functools.partial(kernel, nx, ny), out_shape=jax.ShapeDtyp...]
where the time goes in v3:
time: 39 us; the launch traced here: 38.8 us
  Pallas kernels  37.1 us (95%)
  local copies, waits for them, and re-layouts  1.67 us (4%)
    pallas_call x1, Pallas kernels, body(): pl.pallas_call(functools.partial(kernel, nx, ny), out_shape=jax.ShapeDtyp...  37.1 us
    unnamed x1, local copies, waits for them, and re-layouts  1.67 us

profile of v3, /device:TPU:505, one launch (start us, length us, event | category | flops | bytes accessed | tf_op | source)
XLA Modules:
  0.0 38.8 jit_solution(16381652489676869460)
XLA Ops:
  0.0 37.1 %shard_map.28 = f32[32,2,8,128]{3,2,1,0:T(8,128)} custom-call(f32[4,8,2048]{2,1,0:T(8,128)} %v_hbm.1, f32[8,128]{1,0:T(8,128)} %constant.2.clone.table_hbm), custom_call_target="tpu_custom_call" | custom-call | tf_op jit(solution)/shard_map/pallas_call | solution.py:615
  37.2 1.7 %copy.4 = f32[64,8,128]{2,1,0:T(8,128)} copy(f32[64,8,128]{2,1,0:T(8,128)} %bitcast.1) | data formatting | bytes 524288

commit v4 on v3

--- a/solution.py
+++ b/solution.py
@@ -651,8 +651,8 @@
                 pltpu.SemaphoreType.REGULAR((4,)),
                 pltpu.SemaphoreType.REGULAR,
             ],
-            compiler_params=pltpu.CompilerParams(collective_id=0, has_side_effects=True),
-        )(velocity, jnp.asarray(COLUMNS))
+            compiler_params=pltpu.CompilerParams(collective_id=0, has_side_effects=True, vmem_limit_bytes=24576 * 1024),
+        )(pltpu.with_memory_space_constraint(velocity, pltpu.HBM), pltpu.with_memory_space_constraint(jnp.asarray(COLUMNS), pltpu.HBM))
         return out.reshape(4 * ny, ROWS, TILE)
 
     return jax.shard_map(

time: 39 us -> 37.3 us (0.956)
  local copies, waits for them, and re-layouts: 1.67 us -> 0.71 us
  Pallas kernels: 37.1 us -> 36.4 us
    unnamed x1, local copies, waits for them, and re-layouts: 1.67 us -> 0.71 us
    pallas_call x1, Pallas kernels: 37.1 us -> 36.4 us  [body(): pl.pallas_call(functools.partial(kernel, nx, ny), out_shape=jax.ShapeDtyp...]
where the time goes in v4:
time: 37.3 us; the launch traced here: 37.2 us
  Pallas kernels  36.4 us (98%)
  local copies, waits for them, and re-layouts  0.71 us (2%)
    pallas_call x1, Pallas kernels, body(): pl.pallas_call(functools.partial(kernel, nx, ny), out_shape=jax.ShapeDtyp...  36.4 us

profile of v4, /device:TPU:505, one launch (start us, length us, event | category | flops | bytes accessed | tf_op | source)
XLA Modules:
  0.0 37.2 jit_solution(3315025832476228893)
XLA Ops:
  0.0 36.4 %shard_map.28 = f32[32,2,8,128]{3,2,1,0:T(8,128)S(1)} custom-call(f32[4,8,2048]{2,1,0:T(8,128)} %v_hbm.1, f32[8,128]{1,0:T(8,128)} %constant.2.clone.table_hbm), custom_call_target="tpu_custom_call" | custom-call | tf_op jit(solution)/shard_map/pallas_call | solution.py:615
  36.5 0.7 %copy.4 = f32[64,8,128]{2,1,0:T(8,128)} copy(f32[64,8,128]{2,1,0:T(8,128)S(1)} %bitcast.1) | data formatting | bytes 524288

commit v5 on v4

--- a/solution.py
+++ b/solution.py
@@ -120,7 +120,6 @@
     gx, gy = lax.axis_index("gx"), lax.axis_index("gy")
     half = (gy // 2) % 2
     blocks = ny // 4
-    width = 2 * blocks * TILE
 
     load = pltpu.make_async_copy(v_hbm, v_ref, in_sem.at[0])
     load.start()
@@ -294,7 +293,8 @@
         return halo_copy(n, side, 2 if side is near else 3, beside(STEPS[n]), block)
 
     def block_from_here(i):
-        return lax.rem(gy // 4 + i, blocks)
+        column, back = gy // 4, blocks - 1 - i
+        return lax.rem(column // 2 + back // 2, 2) * 2 + lax.rem(column + back, 2)
 
     came = [wraps(-step) for step in STEPS]
     straight = [jnp.logical_not(flag) for flag in came]
@@ -478,7 +478,8 @@
     def _(i):
         await_halos((0, 1), far, block_from_here(i))
         for j in range(2):
-            block, core, tile = peer(far, 2 * i + j)
+            block, core = block_from_here(i), lax.rem(gy + j, 2)
+            tile = block * 4 + far * 2 + core
             combine(far, block, core, send, tile)
 
             @pl.when(half == 1)

time: 37.3 us -> 37.3 us (level)
  no operation moved by 1% of the time
where the time goes in v5:
time: 37.3 us; the launch traced here: 37.2 us
  Pallas kernels  36.5 us (98%)
  local copies, waits for them, and re-layouts  0.71 us (2%)
    pallas_call x1, Pallas kernels, body(): pl.pallas_call(functools.partial(kernel, nx, ny), out_shape=jax.ShapeDtyp...  36.5 us

profile of v5, /device:TPU:505, one launch (start us, length us, event | category | flops | bytes accessed | tf_op | source)
XLA Modules:
  0.0 37.2 jit_solution(1462761831910985728)
XLA Ops:
  0.0 36.5 %shard_map.28 = f32[32,2,8,128]{3,2,1,0:T(8,128)S(1)} custom-call(f32[4,8,2048]{2,1,0:T(8,128)} %v_hbm.1, f32[8,128]{1,0:T(8,128)} %constant.2.clone.table_hbm), custom_call_target="tpu_custom_call" | custom-call | tf_op jit(solution)/shard_map/pallas_call | solution.py:616
  36.5 0.7 %copy.4 = f32[64,8,128]{2,1,0:T(8,128)} copy(f32[64,8,128]{2,1,0:T(8,128)S(1)} %bitcast.1) | data formatting | bytes 524288

commit v6 on v5

--- a/solution.py
+++ b/solution.py
@@ -114,17 +114,18 @@
     return s * SCALE_LOW, r * SCALE_HIGH
 
 
-def kernel(nx, ny, v_hbm, table_hbm, out_ref, v_ref, table_ref, weights, y_one, y_two, own, own_two, far_two, near_two, go_right,
-           go_left, go_right_two, go_left_two, from_left, from_right, from_left_two, from_right_two, tail_two, send, got,
+def kernel(nx, ny, v_hbm, table_hbm, got, v_ref, table_ref, weights, y_one, y_two, own, own_two, far_two, near_two, go_right,
+           go_left, go_right_two, go_left_two, from_left, from_right, from_left_two, from_right_two, tail_two, send,
            relay, relayed, in_sem, halo_send, halo_recv, send_sem, recv_sem, relay_send, relay_recv, go, ready, join):
     gx, gy = lax.axis_index("gx"), lax.axis_index("gy")
     half = (gy // 2) % 2
     blocks = ny // 4
 
-    load = pltpu.make_async_copy(v_hbm, v_ref, in_sem.at[0])
-    load.start()
-    load_table = pltpu.make_async_copy(table_hbm, table_ref, in_sem.at[1])
+    loads = [pltpu.make_async_copy(v_hbm.at[pl.ds(2 * pair, 2)], v_ref.at[pl.ds(2 * pair, 2)], in_sem.at[pair]) for pair in range(2)]
+    load_table = pltpu.make_async_copy(table_hbm, table_ref, in_sem.at[2])
+    loads[0].start()
     load_table.start()
+    loads[1].start()
 
     other = gy + 2 - 4 * half
 
@@ -182,7 +183,6 @@
     load_table.wait()
     for at in range(len(NAMES)):
         weights[at] = jnp.broadcast_to(table_ref[:, at : at + 1], (ROWS, TILE))
-    load.wait()
 
     lane = lax.broadcasted_iota(jnp.int32, (ROWS, TILE), 1)
     row = lax.broadcasted_iota(jnp.int32, (ROWS, TILE), 0)
@@ -194,6 +194,7 @@
 
     lows = []
     for pair in range(2):
+        loads[pair].wait()
         s, r = swap(v_ref[2 * pair], v_ref[2 * pair + 1], low_lanes(1), 1, 1)
         s, r = lane_lift(s, r, 2)
         y_one[2 * pair] = s
@@ -360,7 +361,7 @@
     pack_two(far)
     late_greetings = jnp.where(wraps(1), 2, jnp.where(wraps(2), 1, 0)) * half
     late_greetings += jnp.where(wraps(-1), 2, jnp.where(wraps(-2), 1, 0)) * jnp.where(heard, 1, 0)
-    near_first = (half == 0) | wraps(8)
+    near_first = (half == 0) | wraps(8) | wraps(-2)
 
     @pl.when(near_first)
     def _():
@@ -383,7 +384,7 @@
                 def _(i):
                     halo_out(n, far, block_from_here(i)).start()
 
-    around = [wraps(step) & (heard if step < 0 else gx >= 0) for step in STEPS]
+    around = [wraps(step) for step in STEPS]
     for n in (2, 0):
         send_far_halos(n, around[n] & jnp.logical_not(answered[n]))
     for n in range(4):
@@ -407,15 +408,15 @@
         x_pass(near)
         pack_two(near)
 
-    late_near = (half == 1) & (lax.rem(gx, 4) == 0) & (gx < 24)
+    late_near = (half == 1) & ((lax.rem(gx, 4) == 0) & (gx < 24)) | (gx == 23)
 
     def send_near_halos(flag):
         for n in range(4):
-            @pl.when(flag & (jnp.logical_not(wraps(STEPS[n])) | ((half == 1) & (STEPS[n] < 0))))
+            @pl.when(flag & jnp.logical_not(wraps(STEPS[n])))
             def _():
                 halo_out(n, near).start()
 
-    send_near_halos(jnp.logical_not(late_near) | wraps(-2))
+    send_near_halos(jnp.logical_not(late_near))
 
     def await_halos(numbers, side, block=None):
         for n in numbers:
@@ -486,7 +487,7 @@
             def _():
                 tile_copy(tile).start()
 
-    send_near_halos(late_near & jnp.logical_not(wraps(-2)))
+    send_near_halos(late_near)
 
     for n in (0, 2):
         @pl.when(answered[n])
@@ -554,11 +555,48 @@
 
     at_ends(take_over, True, False)
 
+    for n in range(4):
+        halo_out(n, near).wait_send()
+    for n in (2, 3):
+        halo_out(n, far).wait_send()
+
+    @pl.loop(0, blocks)
+    def _(i):
+        for n in (0, 1):
+            halo_out(n, far, block_from_here(i)).wait_send()
+
+    @pl.loop(1, 2 * blocks)
+    def _(j):
+        tile_copy(peer(near, j)[2]).wait_send()
+
+    @pl.loop(0, 2 * blocks)
+    def _(j):
+        tile_copy(peer(far, j)[2]).wait_send()
+
+    def drain(low, count):
+        @pl.loop(1, 2 * blocks)
+        def _(j):
+            relay_copy(gy, peer(near, j)[2], count).wait_send()
+
+        if not low:
+            @pl.when(half == 0)
+            def _():
+                @pl.loop(0, 2 * blocks)
+                def _(j):
+                    relay_copy(gy, peer(far, j)[2], count).wait_send()
+
+    at_ends(drain, True, False)
+
+
+def z_kernel(ny, got, out_hbm, out_ref, sems):
     pairs = 2 * ny
     shape = (pairs, ROWS, TILE)
     wide = lax.broadcasted_iota(jnp.int32, (ny, ROWS, TILE), 2) % 2 == 0
     pairs_one = [swap(got[:, n], got[:, n + 1], wide, 1, 2) for n in (0, 2)]
     s, r = leading_lift(*(jnp.stack(both, axis=1).reshape(shape) for both in zip(*pairs_one)))
+    out_ref[1] = r
+    odd_copy = pltpu.make_async_copy(out_ref.at[1], out_hbm.at[:, 1], sems.at[1])
+    odd_copy.start()
     slot = got[:, 4]
     under = pltpu.roll(slot, ROWS - 1, 1)
 
@@ -571,40 +609,11 @@
     low, high = leading_lift(coarse[:, 0], coarse[:, 1])
     coarse = jnp.stack([low, high], axis=1).reshape(shape)
     corner = (lax.broadcasted_iota(jnp.int32, shape, 1) % 2 == 0) & (lax.broadcasted_iota(jnp.int32, shape, 2) % 2 == 0)
-    out_ref[:, 0] = jnp.where(corner, coarse, s)
-    out_ref[:, 1] = r
-
-    for n in range(4):
-        halo_out(n, near).wait_send()
-    for n in (2, 3):
-        halo_out(n, far).wait_send()
-
-    @pl.loop(0, blocks)
-    def _(i):
-        for n in (0, 1):
-            halo_out(n, far, block_from_here(i)).wait_send()
-
-    @pl.loop(1, 2 * blocks)
-    def _(j):
-        tile_copy(peer(near, j)[2]).wait_send()
-
-    @pl.loop(0, 2 * blocks)
-    def _(j):
-        tile_copy(peer(far, j)[2]).wait_send()
-
-    def drain(low, count):
-        @pl.loop(1, 2 * blocks)
-        def _(j):
-            relay_copy(gy, peer(near, j)[2], count).wait_send()
-
-        if not low:
-            @pl.when(half == 0)
-            def _():
-                @pl.loop(0, 2 * blocks)
-                def _(j):
-                    relay_copy(gy, peer(far, j)[2], count).wait_send()
-
-    at_ends(drain, True, False)
+    out_ref[0] = jnp.where(corner, coarse, s)
+    even_copy = pltpu.make_async_copy(out_ref.at[0], out_hbm.at[:, 0], sems.at[0])
+    even_copy.start()
+    odd_copy.wait()
+    even_copy.wait()
 
 
 def solution(mesh):
@@ -613,9 +622,9 @@
     half = length // 2
 
     def body(velocity):
-        out = pl.pallas_call(
+        got = pl.pallas_call(
             functools.partial(kernel, nx, ny),
-            out_shape=jax.ShapeDtypeStruct((2 * ny, 2, ROWS, TILE), F32),
+            out_shape=jax.ShapeDtypeStruct((ny, 5, ROWS, TILE), F32),
             in_specs=[pl.BlockSpec(memory_space=pl.ANY)] * 2,
             out_specs=pl.BlockSpec(memory_space=pltpu.VMEM),
             scratch_shapes=[
@@ -638,10 +647,9 @@
                 pltpu.VMEM((4, ROWS, 2 * TILE), F32),
                 pltpu.VMEM((4, ROWS, half), F32),
                 pltpu.VMEM((ny, 5, ROWS, TILE), F32),
-                pltpu.VMEM((ny, 5, ROWS, TILE), F32),
                 pltpu.VMEM((ny, 3, ROWS, TILE), F32),
                 pltpu.VMEM((ny, 3, ROWS, TILE), F32),
-                pltpu.SemaphoreType.DMA((2,)),
+                pltpu.SemaphoreType.DMA((3,)),
                 pltpu.SemaphoreType.DMA((2, 4 + ny // 2)),
                 pltpu.SemaphoreType.DMA((4, 4 + ny // 2)),
                 pltpu.SemaphoreType.DMA((ny,)),
@@ -654,6 +662,14 @@
             ],
             compiler_params=pltpu.CompilerParams(collective_id=0, has_side_effects=True, vmem_limit_bytes=24576 * 1024),
         )(pltpu.with_memory_space_constraint(velocity, pltpu.HBM), pltpu.with_memory_space_constraint(jnp.asarray(COLUMNS), pltpu.HBM))
+        out = pl.pallas_call(
+            functools.partial(z_kernel, ny),
+            out_shape=jax.ShapeDtypeStruct((2 * ny, 2, ROWS, TILE), F32),
+            in_specs=[pl.BlockSpec(memory_space=pltpu.VMEM)],
+            out_specs=pl.BlockSpec(memory_space=pl.ANY),
+            scratch_shapes=[pltpu.VMEM((2, 2 * ny, ROWS, TILE), F32), pltpu.SemaphoreType.DMA((2,))],
+            compiler_params=pltpu.CompilerParams(vmem_limit_bytes=24 * 2**20),
+        )(got)
         return out.reshape(4 * ny, ROWS, TILE)
 
     return jax.shard_map(

time: 37.3 us -> 37.4 us (level)
  local copies, waits for them, and re-layouts: 0.71 us -> 0 us
  Pallas kernels: 36.5 us -> 37.2 us
    pallas_call x0 -> x1, Pallas kernels: none -> 0.99 us  [body(): pl.pallas_call(functools.partial(z_kernel, ny), out_shape=jax.ShapeDtypeS...]
    unnamed x1 -> x0, local copies, waits for them, and re-layouts: 0.71 us -> none
where the time goes in v6:
time: 37.4 us; the launch traced here: 37.2 us
  Pallas kernels  37.2 us (99%)
    pallas_call x1, Pallas kernels, body(): pl.pallas_call(functools.partial(kernel, nx, ny), out_shape=jax.ShapeDtyp...  36.2 us
    pallas_call x1, Pallas kernels, body(): pl.pallas_call(functools.partial(z_kernel, ny), out_shape=jax.ShapeDtypeS...  0.99 us

profile of v6, /device:TPU:505, one launch (start us, length us, event | category | flops | bytes accessed | tf_op | source)
XLA Modules:
  0.0 37.2 jit_solution(12626654194598169625)
XLA Ops:
  0.0 36.2 %shard_map.28.got = f32[16,5,8,128]{3,2,1,0:T(8,128)S(1)} custom-call(f32[4,8,2048]{2,1,0:T(8,128)} %v_hbm.1, f32[8,128]{1,0:T(8,128)} %constant.2.clone.table_hbm), custom_call_target="tpu_custom_call" | custom-call | tf_op jit(solution)/shard_map/pallas_call | solution.py:625
  36.2 1.0 %shard_map.29 = f32[32,2,8,128]{3,2,1,0:T(8,128)} custom-call(f32[16,5,8,128]{3,2,1,0:T(8,128)S(1)} %shard_map.28.got), custom_call_target="tpu_custom_call" | custom-call | tf_op jit(solution)/shard_map/pallas_call | solution.py:665

commit v7 on v6

--- a/solution.py
+++ b/solution.py
@@ -391,8 +391,16 @@
         @pl.when(around[n])
         def _():
             halo_out(n, near).start()
-    for n in (2, 3, 0, 1):
+    for n in (2, 3):
         send_far_halos(n, jnp.logical_not(around[n]) if STEPS[n] > 0 else gx >= 0)
+
+    @pl.loop(0, blocks)
+    def _(i):
+        halo_out(1, far, block_from_here(i)).start()
+
+        @pl.when(jnp.logical_not(around[0]))
+        def _():
+            halo_out(0, far, block_from_here(i)).start()
 
     @pl.when(half == 1)
     def _():

time: 37.4 us -> 37.4 us (level)
  no operation moved by 1% of the time
where the time goes in v7:
time: 37.4 us; the launch traced here: 37.2 us
  Pallas kernels  37.2 us (99%)
    pallas_call x1, Pallas kernels, body(): pl.pallas_call(functools.partial(kernel, nx, ny), out_shape=jax.ShapeDtyp...  36.2 us
    pallas_call x1, Pallas kernels, body(): pl.pallas_call(functools.partial(z_kernel, ny), out_shape=jax.ShapeDtypeS...  0.99 us

profile of v7, /device:TPU:505, one launch (start us, length us, event | category | flops | bytes accessed | tf_op | source)
XLA Modules:
  0.0 37.2 jit_solution(12027516964519979883)
XLA Ops:
  0.0 36.2 %shard_map.28.got = f32[16,5,8,128]{3,2,1,0:T(8,128)S(1)} custom-call(f32[4,8,2048]{2,1,0:T(8,128)} %v_hbm.1, f32[8,128]{1,0:T(8,128)} %constant.2.clone.table_hbm), custom_call_target="tpu_custom_call" | custom-call | tf_op jit(solution)/shard_map/pallas_call | solution.py:633
  36.2 1.0 %shard_map.29 = f32[32,2,8,128]{3,2,1,0:T(8,128)} custom-call(f32[16,5,8,128]{3,2,1,0:T(8,128)S(1)} %shard_map.28.got), custom_call_target="tpu_custom_call" | custom-call | tf_op jit(solution)/shard_map/pallas_call | solution.py:673

commit v8 on v4

--- a/solution.py
+++ b/solution.py
@@ -122,10 +122,11 @@
     blocks = ny // 4
     width = 2 * blocks * TILE
 
-    load = pltpu.make_async_copy(v_hbm, v_ref, in_sem.at[0])
-    load.start()
-    load_table = pltpu.make_async_copy(table_hbm, table_ref, in_sem.at[1])
+    loads = [pltpu.make_async_copy(v_hbm.at[pl.ds(2 * pair, 2)], v_ref.at[pl.ds(2 * pair, 2)], in_sem.at[pair]) for pair in range(2)]
+    load_table = pltpu.make_async_copy(table_hbm, table_ref, in_sem.at[2])
+    loads[0].start()
     load_table.start()
+    loads[1].start()
 
     other = gy + 2 - 4 * half
 
@@ -183,7 +184,6 @@
     load_table.wait()
     for at in range(len(NAMES)):
         weights[at] = jnp.broadcast_to(table_ref[:, at : at + 1], (ROWS, TILE))
-    load.wait()
 
     lane = lax.broadcasted_iota(jnp.int32, (ROWS, TILE), 1)
     row = lax.broadcasted_iota(jnp.int32, (ROWS, TILE), 0)
@@ -195,6 +195,7 @@
 
     lows = []
     for pair in range(2):
+        loads[pair].wait()
         s, r = swap(v_ref[2 * pair], v_ref[2 * pair + 1], low_lanes(1), 1, 1)
         s, r = lane_lift(s, r, 2)
         y_one[2 * pair] = s
@@ -640,7 +641,7 @@
                 pltpu.VMEM((ny, 5, ROWS, TILE), F32),
                 pltpu.VMEM((ny, 3, ROWS, TILE), F32),
                 pltpu.VMEM((ny, 3, ROWS, TILE), F32),
-                pltpu.SemaphoreType.DMA((2,)),
+                pltpu.SemaphoreType.DMA((3,)),
                 pltpu.SemaphoreType.DMA((2, 4 + ny // 2)),
                 pltpu.SemaphoreType.DMA((4, 4 + ny // 2)),
                 pltpu.SemaphoreType.DMA((ny,)),

time: 37.3 us -> 37.3 us (level)
  no operation moved by 1% of the time
where the time goes in v8:
time: 37.3 us; the launch traced here: 37.2 us
  Pallas kernels  36.5 us (98%)
  local copies, waits for them, and re-layouts  0.71 us (2%)
    pallas_call x1, Pallas kernels, body(): pl.pallas_call(functools.partial(kernel, nx, ny), out_shape=jax.ShapeDtyp...  36.5 us

profile of v8, /device:TPU:505, one launch (start us, length us, event | category | flops | bytes accessed | tf_op | source)
XLA Modules:
  0.0 37.2 jit_solution(8366254812238789099)
XLA Ops:
  0.0 36.5 %shard_map.28 = f32[32,2,8,128]{3,2,1,0:T(8,128)S(1)} custom-call(f32[4,8,2048]{2,1,0:T(8,128)} %v_hbm.1, f32[8,128]{1,0:T(8,128)} %constant.2.clone.table_hbm), custom_call_target="tpu_custom_call" | custom-call | tf_op jit(solution)/shard_map/pallas_call | solution.py:616
  36.5 0.7 %copy.4 = f32[64,8,128]{2,1,0:T(8,128)} copy(f32[64,8,128]{2,1,0:T(8,128)S(1)} %bitcast.1) | data formatting | bytes 524288
